TPU v7x, 32 devices: a whole 2x2x4 slice. The times are simulated.
32 devices in a mesh: ctx: 4 (over z), row: 4 (over x, core), col: 2 (over y).
Axes of the slice: x: 2, y: 2, z: 4, core: 2. Of those that a mesh axis runs over, the one named last changes fastest.
Arguments:
- events: bfloat16 [8192, 4096], P(('ctx', 'row'), 'col'), may hold values from -120 to 120
- domain_ids: int32 [8192], P(('ctx', 'row')), may hold values from 0 to 3
- block_order: int32 [4], replicated, may hold values from 0 to 3, each once
- query_weight: bfloat16 [4096, 4096], P('row', 'col'), may hold values from -0.09375 to 0.09375
- keyval_weight: bfloat16 [4096, 8, 2, 128], P('row'), may hold values from -0.09375 to 0.09375
- head_bias: float32 [32], P('col'), may hold values from -1.5 to 1.5
- out_weight: bfloat16 [4096, 4096], P('row', 'col'), may hold values from -0.09375 to 0.09375
Outputs:
- mixed: bfloat16 [8192, 4096], P(('ctx', 'row'), 'col')
Inputs may be any that keep to these rules, and one draw needn't show every extreme that they name: `block_order`: each index of ctx holds 2048 consecutive events of one block; every place 0 to 3 is named once.
All inputs are finite; a program needn't handle non-finite values.
Results may differ from a plain program's by a relative error of at most 0.0075.
Values may be sent and summed in bfloat16 or wider, within the bound.
A program may use at most 128 MiB of HBM per device.

v0:
```python
import math

import jax
import jax.numpy as jnp
from jax import lax
from jax.sharding import PartitionSpec as P

H = 32
KV = 8
HD = 128


norm_eps = 1e-06
block_rows = 512


def block_place(storage, group_rows, block_order):
    block_index = storage // group_rows
    choices_row = jnp.arange(block_order.shape[0], dtype=jnp.int32)
    looked_up = jnp.sum(
        jnp.where(block_index[:, None] == choices_row[None, :], block_order[None, :], 0), axis=1
    )
    return looked_up * group_rows + storage % group_rows


def shards(events, domain_ids, block_order, query_weight, keyval_weight, head_bias, out_weight):
    row_count = events.shape[0]
    head_count = head_bias.shape[0]
    group_size = H // KV
    pair_heads = max(1, head_count // group_size)
    group_heads = head_count // pair_heads
    group_rows = row_count * lax.axis_size("row")
    scale_factor = 1.0 / math.sqrt(HD)
    whole = lax.all_gather(events, "col", axis=1, tiled=True)
    wide_events = whole.astype(jnp.float32)
    normed = (
        wide_events
        * lax.rsqrt(jnp.mean(wide_events * wide_events, axis=1, keepdims=True) + norm_eps)
    ).astype(jnp.bfloat16)
    pair_start = lax.axis_index("col") * head_count // group_size
    pair_weight = lax.dynamic_slice_in_dim(keyval_weight, pair_start, pair_heads, 1)
    pair_weight = pair_weight.reshape(keyval_weight.shape[0], pair_heads * 2 * HD)
    columns = normed
    query_sums = jnp.dot(
        columns,
        lax.all_gather(query_weight, "row", axis=0, tiled=True),
        preferred_element_type=jnp.float32,
    )
    pair_sums = jnp.dot(
        columns,
        lax.all_gather(pair_weight, "row", axis=0, tiled=True),
        preferred_element_type=jnp.float32,
    )
    queries = query_sums.astype(jnp.bfloat16).reshape(row_count, pair_heads, group_heads, HD)
    keyvals = pair_sums.astype(jnp.bfloat16).reshape(row_count, pair_heads, 2, HD)
    first_row = (lax.axis_index("ctx") * lax.axis_size("row") + lax.axis_index("row")) * row_count
    query_place = block_place(
        first_row + jnp.arange(row_count, dtype=jnp.int32), group_rows, block_order
    )
    inv_count = lax.rsqrt((query_place + 1).astype(jnp.float32))
    head_terms = head_bias.reshape(pair_heads, group_heads)

    def compute_block(running, kv_block, domain_block, key_place):
        scores = (
            jnp.einsum(
                "qkgd,nkd->kgqn", queries, kv_block[:, :, 0, :], preferred_element_type=jnp.float32
            )
            * scale_factor
        )
        same_domain = (domain_ids[:, None] == domain_block[None, :]).astype(jnp.float32)
        scores = scores + head_terms[:, :, None, None] * same_domain[None, None, :, :]
        visible = key_place[None, :] <= query_place[:, None]
        weights = jnp.where(
            visible[None, None, :, :], jax.nn.silu(scores) * inv_count[None, None, :, None], 0.0
        ).astype(jnp.bfloat16)
        return running + jnp.einsum(
            "kgqn,nkd->qkgd", weights, kv_block[:, :, 1, :], preferred_element_type=jnp.float32
        )

    def update(running, kv_block, domain_block, block_first):
        key_place = block_place(
            block_first + jnp.arange(kv_block.shape[0], dtype=jnp.int32), group_rows, block_order
        )
        return compute_block(running, kv_block, domain_block, key_place)

    empty_sums = jnp.zeros((row_count, pair_heads, group_heads, HD), jnp.float32)
    totals = empty_sums
    kv_part = lax.all_gather(keyvals, ("ctx", "row"), axis=0, tiled=True)
    domain_part = lax.all_gather(domain_ids, ("ctx", "row"), axis=0, tiled=True)
    length_rows = kv_part.shape[0]
    number = length_rows // block_rows
    kv_blocks = kv_part.reshape((number, block_rows) + kv_part.shape[1:])
    domain_blocks = domain_part.reshape(number, block_rows)
    firsts = block_rows * jnp.arange(number, dtype=jnp.int32)

    def scan_step(running, block_item):
        return (update(running, block_item[0], block_item[1], block_item[2]), None)

    totals, unused = lax.scan(scan_step, totals, (kv_blocks, domain_blocks, firsts))
    attended = totals
    attended = attended.astype(jnp.bfloat16).reshape(row_count, head_count * HD)
    all_heads = lax.all_gather(attended, "col", axis=1, tiled=True)
    columns = all_heads
    out_sums = jnp.dot(
        columns,
        lax.all_gather(out_weight, "row", axis=0, tiled=True),
        preferred_element_type=jnp.float32,
    )
    return out_sums.astype(jnp.bfloat16)


def solution(mesh):
    in_specs = (
        P(("ctx", "row"), "col"),
        P(("ctx", "row")),
        P(),
        P("row", "col"),
        P("row", None, None, None),
        P("col"),
        P("row", "col"),
    )
    out_specs = P(("ctx", "row"), "col")
    return jax.shard_map(shards, mesh=mesh, in_specs=in_specs, out_specs=out_specs, check_vma=False)
```

profile of v0, /device:TPU:27, one launch (start us, length us, event | category | flops | bytes accessed | tf_op | source)
XLA Modules:
  0.0 678.5 jit_solution(14346082509125235298)
XLA Ops:
  6.5 0.7 all-gather.8.cloned.1.call-update
  7.3 3.0 constant_dynamic-slice_fusion.2
  10.4 2.7 reshape.142
  13.1 0.7 all-gather.14.cloned.1.call-update
  13.9 52.8 %all-gather.8.cloned.1.call-done = bf16[512,4096]{1,0:T(8,128)(2,1)} async-done(((bf16[512,2048]{1,0:T(8,128)(2,1)}), bf16[512,4096]{1,0:T(8,128)(2,1)}) %all-gather.8.cloned.1.call-update) | async-done | bytes 4194320 | tf_op jit(solution)/shard_map/all_gather | solution.py:34
  66.6 3.1 fusion.8
  69.7 56.3 %all-gather.10.cloned.1.call-done = bf16[4096,1024]{1,0:T(8,128)(2,1)} async-done(((bf16[1024,1024]{1,0:T(8,128)(2,1)}), bf16[4096,1024]{1,0:T(8,128)(2,1)}) %all-gather.10.cloned.1.call-update) | async-done | bytes 8388624 | tf_op jit(solution)/shard_map/all_gather | solution.py:51
  126.0 9.2 %fusion.13 = bf16[512,1024]{1,0:T(8,128)(2,1)S(1)} fusion(bf16[4096,1024]{1,0:T(8,128)(2,1)} %all-gather.10.cloned.1.call-done, bf16[512,4096]{1,0:T(8,128)(2,1)} %all-gather.8.cloned.1.call-done, f32[512]{0:T(512)S(1)} %add_rsqrt_fusion), kind=kOutput, calls=%fused_computation.34 | convolution fusion | flops 4301783040 | bytes 13633536 | tf_op jit(solution)/shard_map/dot_general | solution.py:49
  135.2 0.8 reshape.143
  136.0 1.1 copy.23
  138.0 17.0 %all-gather = s32[16,1,512]{2,1,0:T(1,128)S(1)} all-gather(s32[1,1,512]{2,1,0:T(1,128)S(1)} %bitcast.58), channel_id=1, replica_groups=mesh['ctx'=4,'row'=4,'col'=2] {'ctx','row'}, dimensions={0}, use_global_device_ids=true | all-gather | bytes 34816 | tf_op jit(solution)/shard_map/all_gather | solution.py:89
  154.9 78.9 %all-gather.14.cloned.1.call-done = bf16[4096,2048]{1,0:T(8,128)(2,1)} async-done(((bf16[1024,2048]{1,0:T(8,128)(2,1)}), bf16[4096,2048]{1,0:T(8,128)(2,1)}) %all-gather.14.cloned.1.call-update) | async-done | bytes 16777232 | tf_op jit(solution)/shard_map/all_gather | solution.py:46
  233.9 14.6 %convolution_convert_fusion.1 = bf16[512,2048]{1,0:T(8,128)(2,1)} fusion(bf16[4096,2048]{1,0:T(8,128)(2,1)} %all-gather.14.cloned.1.call-done, bf16[512,4096]{1,0:T(8,128)(2,1)} %all-gather.8.cloned.1.call-done, f32[512]{0:T(512)S(1)} %add_rsqrt_fusion), kind=kOutput, calls=%fused_computation.32 | convolution fusion | flops 8597274624 | bytes 23070720 | tf_op jit(solution)/shard_map/dot_general | solution.py:44
  248.5 3.2 reshape.145
  251.7 1.9 copy.25
  253.6 107.2 %all-gather.12.cloned.1.call-done = bf16[8192,4,2,128]{3,0,2,1:T(8,128)(2,1)} async-done(((bf16[512,4,2,128]{3,0,2,1:T(8,128)(2,1)}), bf16[8192,4,2,128]{3,0,2,1:T(8,128)(2,1)}) %all-gather.12.cloned.1.call-update) | async-done | bytes 16777232 | tf_op jit(solution)/shard_map/all_gather | solution.py:88
  360.8 235.0 %while.13 = (s32[]{:T(128)}, f32[512,4,4,128]{0,3,2,1:T(8,128)}, bf16[16,512,4,2,128]{4,1,0,3,2:T(8,128)(2,1)}, s32[16]{0:T(128)S(1)}, s32[4]{0:T(128)S(1)}, /*i...) while((s32[]{:T(128)}, f32[512,4,4,128]{0,3,2,1:T(8,128)}, ...), condition=%wide.region_4.5_spmd.clone, body=%wide.region_2.4_spmd.clone.sunk | while | flops 2192331264 | bytes 16278383 | solution.py:99
  360.8 0.6 dynamic_slice.40
  363.1 1.3 copy_bitcast_fusion.3
  364.5 10.2 %bitcast_add_fusion.3 = f32[512,4,4,128]{0,3,2,1:T(8,128)} fusion(f32[512,4,4,128]{0,3,2,1:T(8,128)} %get-tuple-element.337, pred[]{:T(512)S(6)} %compare.25, bf16[512,4,4,128]{3,0,2,1:T(8,128)(2,1)} %get-tuple-element.355, f32[512]{0:T(512)S(1)} %get-tuple-element.359, f32[512,512]{0,1:T(8,128)S(1)} %get-tuple-element.321, f32[4,4]{1,0:T(4,128)S(1)} %mul.183, ...), kind=kOutput, calls=%fused_computation.2.clone.1 | convolution fusion | flops 2191523840 | bytes 12847169 | tf_op jit(solution)/shard_map/while/body/eval_jaxpr/kgqn,nkd->qkgd/dot_general | solution.py:76
  374.8 0.6 dynamic_slice.40
  377.1 1.6 copy_bitcast_fusion.3
  378.8 11.5 %bitcast_add_fusion.3 = f32[512,4,4,128]{0,3,2,1:T(8,128)} fusion(f32[512,4,4,128]{0,3,2,1:T(8,128)} %get-tuple-element.337, pred[]{:T(512)S(6)} %compare.25, bf16[512,4,4,128]{3,0,2,1:T(8,128)(2,1)} %get-tuple-element.355, f32[512]{0:T(512)S(1)} %get-tuple-element.359, f32[512,512]{0,1:T(8,128)S(1)} %get-tuple-element.321, f32[4,4]{1,0:T(4,128)S(1)} %mul.183, ...), kind=kOutput, calls=%fused_computation.2.clone.1 | convolution fusion | flops 2191523840 | bytes 12847169 | tf_op jit(solution)/shard_map/while/body/eval_jaxpr/kgqn,nkd->qkgd/dot_general | solution.py:76
  390.4 0.6 dynamic_slice.40
  392.7 1.3 copy_bitcast_fusion.3
  394.1 10.9 %bitcast_add_fusion.3 = f32[512,4,4,128]{0,3,2,1:T(8,128)} fusion(f32[512,4,4,128]{0,3,2,1:T(8,128)} %get-tuple-element.337, pred[]{:T(512)S(6)} %compare.25, bf16[512,4,4,128]{3,0,2,1:T(8,128)(2,1)} %get-tuple-element.355, f32[512]{0:T(512)S(1)} %get-tuple-element.359, f32[512,512]{0,1:T(8,128)S(1)} %get-tuple-element.321, f32[4,4]{1,0:T(4,128)S(1)} %mul.183, ...), kind=kOutput, calls=%fused_computation.2.clone.1 | convolution fusion | flops 2191523840 | bytes 12847169 | tf_op jit(solution)/shard_map/while/body/eval_jaxpr/kgqn,nkd->qkgd/dot_general | solution.py:76
  405.0 0.6 dynamic_slice.40
  407.4 1.3 copy_bitcast_fusion.3
  408.8 10.9 %bitcast_add_fusion.3 = f32[512,4,4,128]{0,3,2,1:T(8,128)} fusion(f32[512,4,4,128]{0,3,2,1:T(8,128)} %get-tuple-element.337, pred[]{:T(512)S(6)} %compare.25, bf16[512,4,4,128]{3,0,2,1:T(8,128)(2,1)} %get-tuple-element.355, f32[512]{0:T(512)S(1)} %get-tuple-element.359, f32[512,512]{0,1:T(8,128)S(1)} %get-tuple-element.321, f32[4,4]{1,0:T(4,128)S(1)} %mul.183, ...), kind=kOutput, calls=%fused_computation.2.clone.1 | convolution fusion | flops 2191523840 | bytes 12847169 | tf_op jit(solution)/shard_map/while/body/eval_jaxpr/kgqn,nkd->qkgd/dot_general | solution.py:76
  419.7 0.6 dynamic_slice.40
  422.0 1.3 copy_bitcast_fusion.3
  423.4 10.9 %bitcast_add_fusion.3 = f32[512,4,4,128]{0,3,2,1:T(8,128)} fusion(f32[512,4,4,128]{0,3,2,1:T(8,128)} %get-tuple-element.337, pred[]{:T(512)S(6)} %compare.25, bf16[512,4,4,128]{3,0,2,1:T(8,128)(2,1)} %get-tuple-element.355, f32[512]{0:T(512)S(1)} %get-tuple-element.359, f32[512,512]{0,1:T(8,128)S(1)} %get-tuple-element.321, f32[4,4]{1,0:T(4,128)S(1)} %mul.183, ...), kind=kOutput, calls=%fused_computation.2.clone.1 | convolution fusion | flops 2191523840 | bytes 12847169 | tf_op jit(solution)/shard_map/while/body/eval_jaxpr/kgqn,nkd->qkgd/dot_general | solution.py:76
  434.4 0.6 dynamic_slice.40
  436.7 1.3 copy_bitcast_fusion.3
  438.1 10.9 %bitcast_add_fusion.3 = f32[512,4,4,128]{0,3,2,1:T(8,128)} fusion(f32[512,4,4,128]{0,3,2,1:T(8,128)} %get-tuple-element.337, pred[]{:T(512)S(6)} %compare.25, bf16[512,4,4,128]{3,0,2,1:T(8,128)(2,1)} %get-tuple-element.355, f32[512]{0:T(512)S(1)} %get-tuple-element.359, f32[512,512]{0,1:T(8,128)S(1)} %get-tuple-element.321, f32[4,4]{1,0:T(4,128)S(1)} %mul.183, ...), kind=kOutput, calls=%fused_computation.2.clone.1 | convolution fusion | flops 2191523840 | bytes 12847169 | tf_op jit(solution)/shard_map/while/body/eval_jaxpr/kgqn,nkd->qkgd/dot_general | solution.py:76
  449.0 0.6 dynamic_slice.40
  451.4 1.3 copy_bitcast_fusion.3
  452.8 10.9 %bitcast_add_fusion.3 = f32[512,4,4,128]{0,3,2,1:T(8,128)} fusion(f32[512,4,4,128]{0,3,2,1:T(8,128)} %get-tuple-element.337, pred[]{:T(512)S(6)} %compare.25, bf16[512,4,4,128]{3,0,2,1:T(8,128)(2,1)} %get-tuple-element.355, f32[512]{0:T(512)S(1)} %get-tuple-element.359, f32[512,512]{0,1:T(8,128)S(1)} %get-tuple-element.321, f32[4,4]{1,0:T(4,128)S(1)} %mul.183, ...), kind=kOutput, calls=%fused_computation.2.clone.1 | convolution fusion | flops 2191523840 | bytes 12847169 | tf_op jit(solution)/shard_map/while/body/eval_jaxpr/kgqn,nkd->qkgd/dot_general | solution.py:76
  463.7 0.6 dynamic_slice.40
  466.0 1.4 copy_bitcast_fusion.3
  467.5 10.9 %bitcast_add_fusion.3 = f32[512,4,4,128]{0,3,2,1:T(8,128)} fusion(f32[512,4,4,128]{0,3,2,1:T(8,128)} %get-tuple-element.337, pred[]{:T(512)S(6)} %compare.25, bf16[512,4,4,128]{3,0,2,1:T(8,128)(2,1)} %get-tuple-element.355, f32[512]{0:T(512)S(1)} %get-tuple-element.359, f32[512,512]{0,1:T(8,128)S(1)} %get-tuple-element.321, f32[4,4]{1,0:T(4,128)S(1)} %mul.183, ...), kind=kOutput, calls=%fused_computation.2.clone.1 | convolution fusion | flops 2191523840 | bytes 12847169 | tf_op jit(solution)/shard_map/while/body/eval_jaxpr/kgqn,nkd->qkgd/dot_general | solution.py:76
  478.4 0.6 dynamic_slice.40
  480.8 1.3 copy_bitcast_fusion.3
  482.2 10.9 %bitcast_add_fusion.3 = f32[512,4,4,128]{0,3,2,1:T(8,128)} fusion(f32[512,4,4,128]{0,3,2,1:T(8,128)} %get-tuple-element.337, pred[]{:T(512)S(6)} %compare.25, bf16[512,4,4,128]{3,0,2,1:T(8,128)(2,1)} %get-tuple-element.355, f32[512]{0:T(512)S(1)} %get-tuple-element.359, f32[512,512]{0,1:T(8,128)S(1)} %get-tuple-element.321, f32[4,4]{1,0:T(4,128)S(1)} %mul.183, ...), kind=kOutput, calls=%fused_computation.2.clone.1 | convolution fusion | flops 2191523840 | bytes 12847169 | tf_op jit(solution)/shard_map/while/body/eval_jaxpr/kgqn,nkd->qkgd/dot_general | solution.py:76
  493.1 0.6 dynamic_slice.40
  495.4 1.3 copy_bitcast_fusion.3
  496.8 10.9 %bitcast_add_fusion.3 = f32[512,4,4,128]{0,3,2,1:T(8,128)} fusion(f32[512,4,4,128]{0,3,2,1:T(8,128)} %get-tuple-element.337, pred[]{:T(512)S(6)} %compare.25, bf16[512,4,4,128]{3,0,2,1:T(8,128)(2,1)} %get-tuple-element.355, f32[512]{0:T(512)S(1)} %get-tuple-element.359, f32[512,512]{0,1:T(8,128)S(1)} %get-tuple-element.321, f32[4,4]{1,0:T(4,128)S(1)} %mul.183, ...), kind=kOutput, calls=%fused_computation.2.clone.1 | convolution fusion | flops 2191523840 | bytes 12847169 | tf_op jit(solution)/shard_map/while/body/eval_jaxpr/kgqn,nkd->qkgd/dot_general | solution.py:76
  510.1 1.3 copy_bitcast_fusion.3
  511.5 10.9 %bitcast_add_fusion.3 = f32[512,4,4,128]{0,3,2,1:T(8,128)} fusion(f32[512,4,4,128]{0,3,2,1:T(8,128)} %get-tuple-element.337, pred[]{:T(512)S(6)} %compare.25, bf16[512,4,4,128]{3,0,2,1:T(8,128)(2,1)} %get-tuple-element.355, f32[512]{0:T(512)S(1)} %get-tuple-element.359, f32[512,512]{0,1:T(8,128)S(1)} %get-tuple-element.321, f32[4,4]{1,0:T(4,128)S(1)} %mul.183, ...), kind=kOutput, calls=%fused_computation.2.clone.1 | convolution fusion | flops 2191523840 | bytes 12847169 | tf_op jit(solution)/shard_map/while/body/eval_jaxpr/kgqn,nkd->qkgd/dot_general | solution.py:76
  522.4 0.6 dynamic_slice.40
  524.8 1.3 copy_bitcast_fusion.3
  526.2 10.9 %bitcast_add_fusion.3 = f32[512,4,4,128]{0,3,2,1:T(8,128)} fusion(f32[512,4,4,128]{0,3,2,1:T(8,128)} %get-tuple-element.337, pred[]{:T(512)S(6)} %compare.25, bf16[512,4,4,128]{3,0,2,1:T(8,128)(2,1)} %get-tuple-element.355, f32[512]{0:T(512)S(1)} %get-tuple-element.359, f32[512,512]{0,1:T(8,128)S(1)} %get-tuple-element.321, f32[4,4]{1,0:T(4,128)S(1)} %mul.183, ...), kind=kOutput, calls=%fused_computation.2.clone.1 | convolution fusion | flops 2191523840 | bytes 12847169 | tf_op jit(solution)/shard_map/while/body/eval_jaxpr/kgqn,nkd->qkgd/dot_general | solution.py:76
  539.4 1.3 copy_bitcast_fusion.3
  540.8 10.9 %bitcast_add_fusion.3 = f32[512,4,4,128]{0,3,2,1:T(8,128)} fusion(f32[512,4,4,128]{0,3,2,1:T(8,128)} %get-tuple-element.337, pred[]{:T(512)S(6)} %compare.25, bf16[512,4,4,128]{3,0,2,1:T(8,128)(2,1)} %get-tuple-element.355, f32[512]{0:T(512)S(1)} %get-tuple-element.359, f32[512,512]{0,1:T(8,128)S(1)} %get-tuple-element.321, f32[4,4]{1,0:T(4,128)S(1)} %mul.183, ...), kind=kOutput, calls=%fused_computation.2.clone.1 | convolution fusion | flops 2191523840 | bytes 12847169 | tf_op jit(solution)/shard_map/while/body/eval_jaxpr/kgqn,nkd->qkgd/dot_general | solution.py:76
  554.1 1.3 copy_bitcast_fusion.3
  555.5 10.9 %bitcast_add_fusion.3 = f32[512,4,4,128]{0,3,2,1:T(8,128)} fusion(f32[512,4,4,128]{0,3,2,1:T(8,128)} %get-tuple-element.337, pred[]{:T(512)S(6)} %compare.25, bf16[512,4,4,128]{3,0,2,1:T(8,128)(2,1)} %get-tuple-element.355, f32[512]{0:T(512)S(1)} %get-tuple-element.359, f32[512,512]{0,1:T(8,128)S(1)} %get-tuple-element.321, f32[4,4]{1,0:T(4,128)S(1)} %mul.183, ...), kind=kOutput, calls=%fused_computation.2.clone.1 | convolution fusion | flops 2191523840 | bytes 12847169 | tf_op jit(solution)/shard_map/while/body/eval_jaxpr/kgqn,nkd->qkgd/dot_general | solution.py:76
  566.4 0.6 dynamic_slice.40
  568.8 1.3 copy_bitcast_fusion.3
  570.2 10.9 %bitcast_add_fusion.3 = f32[512,4,4,128]{0,3,2,1:T(8,128)} fusion(f32[512,4,4,128]{0,3,2,1:T(8,128)} %get-tuple-element.337, pred[]{:T(512)S(6)} %compare.25, bf16[512,4,4,128]{3,0,2,1:T(8,128)(2,1)} %get-tuple-element.355, f32[512]{0:T(512)S(1)} %get-tuple-element.359, f32[512,512]{0,1:T(8,128)S(1)} %get-tuple-element.321, f32[4,4]{1,0:T(4,128)S(1)} %mul.183, ...), kind=kOutput, calls=%fused_computation.2.clone.1 | convolution fusion | flops 2191523840 | bytes 12847169 | tf_op jit(solution)/shard_map/while/body/eval_jaxpr/kgqn,nkd->qkgd/dot_general | solution.py:76
  583.5 1.3 copy_bitcast_fusion.3
  584.9 10.9 %bitcast_add_fusion.3 = f32[512,4,4,128]{0,3,2,1:T(8,128)} fusion(f32[512,4,4,128]{0,3,2,1:T(8,128)} %get-tuple-element.337, pred[]{:T(512)S(6)} %compare.25, bf16[512,4,4,128]{3,0,2,1:T(8,128)(2,1)} %get-tuple-element.355, f32[512]{0:T(512)S(1)} %get-tuple-element.359, f32[512,512]{0,1:T(8,128)S(1)} %get-tuple-element.321, f32[4,4]{1,0:T(4,128)S(1)} %mul.183, ...), kind=kOutput, calls=%fused_computation.2.clone.1 | convolution fusion | flops 2191523840 | bytes 12847169 | tf_op jit(solution)/shard_map/while/body/eval_jaxpr/kgqn,nkd->qkgd/dot_general | solution.py:76
  595.8 3.8 convert_element_type.42
  599.6 57.5 %all-gather.16.cloned.1.call-done = bf16[512,4096]{0,1:T(8,128)(2,1)} async-done(((bf16[512,2048]{0,1:T(8,128)(2,1)}), bf16[512,4096]{0,1:T(8,128)(2,1)}) %all-gather.16.cloned.1.call-update) | async-done | bytes 4194320 | tf_op jit(solution)/shard_map/all_gather | solution.py:102
  657.1 14.6 %convolution_convert_fusion = bf16[512,2048]{1,0:T(8,128)(2,1)} fusion(bf16[512,4096]{0,1:T(8,128)(2,1)} %all-gather.16.cloned.1.call-done, bf16[4096,2048]{1,0:T(8,128)(2,1)} %all-gather.18.cloned.1.call-done), kind=kOutput, calls=%fused_computation.31 | convolution fusion | flops 8590983168 | bytes 23068672 | tf_op jit(solution)/shard_map/dot_general | solution.py:104
  (124 shorter events, 31.4 us)
Async XLA Ops:
  6.5 60.1 %all-gather.8.cloned.1.call-start = ((), (), s32[]{:S(2)}) async-start(), calls=%async_computation | async-start | bytes 6291456 | tf_op jit(solution)/shard_map/all_gather | solution.py:34
  7.3 118.8 %all-gather.10.cloned.1.call-start = ((), (), s32[]{:S(2)}) async-start(), calls=%async_computation.1 | async-start | bytes 10485760 | tf_op jit(solution)/shard_map/all_gather | solution.py:51
  13.1 220.8 %all-gather.14.cloned.1.call-start = ((), (), s32[]{:S(2)}) async-start(), calls=%async_computation.3 | async-start | bytes 20971520 | tf_op jit(solution)/shard_map/all_gather | solution.py:46
  13.8 347.0 %all-gather.12.cloned.1.call-start = ((), (), s32[]{:S(2)}) async-start(), calls=%async_computation.2 | async-start | bytes 17825792 | tf_op jit(solution)/shard_map/all_gather | solution.py:88
  136.0 1.8 copy-start.1
  136.0 2.0 copy-start
  137.2 462.5 %all-gather.18.cloned.1.call-start = ((), (), s32[]{:S(2)}) async-start(), calls=%async_computation.5 | async-start | bytes 20971520 | tf_op jit(solution)/shard_map/all_gather | solution.py:106
  137.8 519.3 %all-gather.16.cloned.1.call-start = ((), (), s32[]{:S(2)}) async-start(), calls=%async_computation.4 | async-start | bytes 6291456 | tf_op jit(solution)/shard_map/all_gather | solution.py:102
  248.5 112.3 %copy-start.2 = (f32[16]{0:T(128)S(1)}, f32[16]{0:T(128)}, u32[]{:S(2)}) copy-start(f32[16]{0:T(128)} %param.14) | copy-start | bytes 196
Sparse Core Ops, SparseCore 0:
  8.9 57.6 all-gather.7
  68.2 57.7 all-gather.9
  127.6 106.2 all-gather.13
  235.9 124.8 all-gather.11
  362.2 106.1 all-gather.17
  599.7 57.3 all-gather.15
where the time goes:
time: 681 us; the launch traced here: 679 us
  waiting for transfers between devices  355 us (52%)
  matrix products  213 us (31%)
  local copies, waits for them, and re-layouts  45.9 us (7%)
  other arithmetic  33.4 us (5%)
  blocking collectives  17 us (2%)
  between operations  13.6 us (2%)
    dot_general x16, matrix products, compute_block(): jnp.einsum('kgqn,nkd->qkgd', weights, kv_block[:, :, 1, :], preferred_ele...  175 us
    all_gather x1, waiting for transfers between devices, shards(): kv_part = lax.all_gather(keyvals, ('ctx', 'row'), axis=0, tiled=True)  107 us
    all_gather x1, waiting for transfers between devices, shards(): lax.all_gather(query_weight, 'row', axis=0, tiled=True)  78.9 us
    all_gather x1, waiting for transfers between devices, shards(): all_heads = lax.all_gather(attended, 'col', axis=1, tiled=True)  57.5 us
    all_gather x1, waiting for transfers between devices, shards(): lax.all_gather(pair_weight, 'row', axis=0, tiled=True)  56.3 us
    all_gather x1, waiting for transfers between devices, shards(): whole = lax.all_gather(events, 'col', axis=1, tiled=True)  52.8 us
    squeeze x16, local copies, waits for them, and re-layouts, shards(): lax.scan(scan_step, totals, (kv_blocks, domain_blocks, firsts))  21.3 us
    all_gather x1, blocking collectives, shards(): domain_part = lax.all_gather(domain_ids, ('ctx', 'row'), axis=0, tiled=True)  17 us
  transfers between devices with their start and end apart: 6, of which 5 were waited for; matrix products, arithmetic and copies ran while one was open for 41% of the time, Pallas kernels for 0%

commit v1 on v0

v1 whole, which is shorter than its diff:
```python
import functools
import math

import jax
import jax.numpy as jnp
from jax import lax
from jax.experimental import pallas as pl
from jax.experimental.pallas import tpu as pltpu
from jax.sharding import PartitionSpec as P

H = 32
KV = 8
HD = 128
LANES = 128
HALF = 32

norm_eps = 1e-06


def block_place(storage, group_rows, block_order):
    block_index = storage // group_rows
    choices_row = jnp.arange(block_order.shape[0], dtype=jnp.int32)
    looked_up = jnp.sum(
        jnp.where(block_index[:, None] == choices_row[None, :], block_order[None, :], 0), axis=1
    )
    return looked_up * group_rows + storage % group_rows


def attention_body(kind_ref, q_ref, kv_ref, qhot_ref, khot_ref, bias_ref, inv_ref, o_ref, qa, ka, acc):
    step = pl.program_id(1)
    group_heads = q_ref.shape[1] // HD
    kind = kind_ref[step]

    @pl.when(step == 0)
    def _():
        acc[...] = jnp.zeros_like(acc)
        for h in range(group_heads):
            qa[h, :, :HD] = q_ref[:, h * HD:(h + 1) * HD]
            qa[h, :, HD:] = (qhot_ref[...] * bias_ref[0, h:h + 1, :]).astype(jnp.bfloat16)

    def tile(diagonal):
        ka[:, :HD] = kv_ref[:, :HD]
        ka[:, HD:] = khot_ref[...]
        for h in range(group_heads):
            half = lax.dot_general(
                qa[h], ka[...], (((1,), (1,)), ((), ())), preferred_element_type=jnp.float32
            )
            w = half * jnp.tanh(half) + half
            if diagonal:
                ti = lax.broadcasted_iota(jnp.int32, w.shape, 0)
                ui = lax.broadcasted_iota(jnp.int32, w.shape, 1)
                w = jnp.where(ui <= ti, w, 0.0)
            acc[h] += jnp.dot(
                w.astype(jnp.bfloat16), kv_ref[:, HD:], preferred_element_type=jnp.float32
            )

    @pl.when(kind == 1)
    def _():
        tile(False)

    @pl.when(kind == 2)
    def _():
        tile(True)

    @pl.when(step == pl.num_programs(1) - 1)
    def _():
        for h in range(group_heads):
            o_ref[:, h * HD:(h + 1) * HD] = (acc[h] * inv_ref[...]).astype(jnp.bfloat16)


def attention(kinds, queries, kv_all, query_hot, key_hot, bias_lanes, inv_count):
    rows, width = queries.shape
    pair_heads, group_heads, _ = bias_lanes.shape
    tiles = kinds.shape[0]
    gw = group_heads * HD
    return pl.pallas_call(
        attention_body,
        grid_spec=pltpu.PrefetchScalarGridSpec(
            num_scalar_prefetch=1,
            grid=(pair_heads, tiles),
            in_specs=[
                pl.BlockSpec((rows, gw), lambda g, j, k: (0, g)),
                pl.BlockSpec((rows, 2 * HD), lambda g, j, k: (j, g)),
                pl.BlockSpec((rows, LANES), lambda g, j, k: (0, 0)),
                pl.BlockSpec((rows, LANES), lambda g, j, k: (j, 0)),
                pl.BlockSpec((1, group_heads, LANES), lambda g, j, k: (g, 0, 0)),
                pl.BlockSpec((rows, 1), lambda g, j, k: (0, 0)),
            ],
            out_specs=pl.BlockSpec((rows, gw), lambda g, j, k: (0, g)),
            scratch_shapes=[
                pltpu.VMEM((group_heads, rows, 2 * HD), jnp.bfloat16),
                pltpu.VMEM((rows, 2 * HD), jnp.bfloat16),
                pltpu.VMEM((group_heads, rows, HD), jnp.float32),
            ],
        ),
        out_shape=jax.ShapeDtypeStruct((rows, width), jnp.bfloat16),
        compiler_params=pltpu.CompilerParams(vmem_limit_bytes=48 * 1024 * 1024),
        cost_estimate=pl.CostEstimate(
            flops=4 * rows * rows * tiles * width, bytes_accessed=rows * tiles * 1024 * 2,
            transcendentals=rows * rows * tiles * width // HD,
        ),
    )(kinds, queries, kv_all, query_hot, key_hot, bias_lanes, inv_count)


def hot_lanes(domains):
    lane = lax.broadcasted_iota(jnp.int32, (1, LANES), 1)
    return ((lane % HALF == domains[:, None]) & (lane < 2 * HALF)).astype(jnp.bfloat16)


def shards(events, domain_ids, block_order, query_weight, keyval_weight, head_bias, out_weight):
    row_count = events.shape[0]
    head_count = head_bias.shape[0]
    group_size = H // KV
    pair_heads = max(1, head_count // group_size)
    group_heads = head_count // pair_heads
    rows_axis = lax.axis_size("row")
    group_rows = row_count * rows_axis
    scale_factor = 1.0 / math.sqrt(HD)
    whole = lax.all_gather(events, "col", axis=1, tiled=True)
    wide_events = whole.astype(jnp.float32)
    normed = (
        wide_events
        * lax.rsqrt(jnp.mean(wide_events * wide_events, axis=1, keepdims=True) + norm_eps)
    ).astype(jnp.bfloat16)
    pair_start = lax.axis_index("col") * head_count // group_size
    pair_weight = lax.dynamic_slice_in_dim(keyval_weight, pair_start, pair_heads, 1)
    pair_weight = pair_weight.reshape(keyval_weight.shape[0], pair_heads * 2 * HD)
    pair_sums = jnp.dot(
        normed,
        lax.all_gather(pair_weight, "row", axis=0, tiled=True),
        preferred_element_type=jnp.float32,
    )
    query_sums = jnp.dot(
        normed,
        lax.all_gather(query_weight, "row", axis=0, tiled=True),
        preferred_element_type=jnp.float32,
    )
    queries = (query_sums * (0.5 * scale_factor)).astype(jnp.bfloat16)
    keyvals = pair_sums.astype(jnp.bfloat16)
    first_row = (lax.axis_index("ctx") * rows_axis + lax.axis_index("row")) * row_count
    query_place = block_place(
        first_row + jnp.arange(row_count, dtype=jnp.int32), group_rows, block_order
    )
    inv_count = lax.rsqrt((query_place + 1).astype(jnp.float32))[:, None]
    half_bias = 0.5 * head_bias
    high = half_bias.astype(jnp.bfloat16).astype(jnp.float32)
    low = half_bias - high
    lane = jnp.arange(LANES, dtype=jnp.int32)[None, :]
    bias_lanes = jnp.where(lane < HALF, high[:, None], jnp.where(lane < 2 * HALF, low[:, None], 0.0))
    bias_lanes = bias_lanes.reshape(pair_heads, group_heads, LANES)
    kv_all = lax.all_gather(keyvals, ("ctx", "row"), axis=0, tiled=True)
    domain_all = lax.all_gather(domain_ids, ("ctx", "row"), axis=0, tiled=True)
    tiles = kv_all.shape[0] // row_count
    tile_first = block_place(
        row_count * jnp.arange(tiles, dtype=jnp.int32), group_rows, block_order
    )
    kinds = jnp.where(
        tile_first < query_place[0], 1, jnp.where(tile_first == query_place[0], 2, 0)
    ).astype(jnp.int32)
    attended = attention(
        kinds, queries, kv_all, hot_lanes(domain_ids), hot_lanes(domain_all), bias_lanes, inv_count
    )
    all_heads = lax.all_gather(attended, "col", axis=1, tiled=True)
    out_sums = jnp.dot(
        all_heads,
        lax.all_gather(out_weight, "row", axis=0, tiled=True),
        preferred_element_type=jnp.float32,
    )
    return out_sums.astype(jnp.bfloat16)


def solution(mesh):
    in_specs = (
        P(("ctx", "row"), "col"),
        P(("ctx", "row")),
        P(),
        P("row", "col"),
        P("row", None, None, None),
        P("col"),
        P("row", "col"),
    )
    out_specs = P(("ctx", "row"), "col")
    return jax.shard_map(shards, mesh=mesh, in_specs=in_specs, out_specs=out_specs, check_vma=False)
```

time: 681 us -> 551 us (0.81)
  matrix products: 213 us -> 38.4 us
  waiting for transfers between devices: 355 us -> 410 us
  Pallas kernels: 0 us -> 53.4 us
  local copies, waits for them, and re-layouts: 45.9 us -> 6.62 us
  other arithmetic: 33.4 us -> 8.86 us
    dot_general x19 -> x3, matrix products: 213 us -> 38.4 us  [the longest x1 14.5 us: shards(): jnp.dot(all_heads, lax.all_gather(out_weight, 'row', axis=0, tiled=True),...]
    all_gather x1, waiting for transfers between devices: 0.02 us -> 54.2 us  [shards(): lax.all_gather(out_weight, 'row', axis=0, tiled=True)]
    pallas_call x0 -> x1, Pallas kernels: none -> 53.4 us  [attention(): pl.pallas_call(attention_body, grid_spec=pltpu.PrefetchScalarGridSpec(num...]
    squeeze x16 -> x0, local copies, waits for them, and re-layouts: 21.3 us -> none  [shards(): lax.scan(scan_step, totals, (kv_blocks, domain_blocks, firsts))]
    dynamic_slice x32 -> x0, local copies, waits for them, and re-layouts: 10.6 us -> none  [shards(): lax.scan(scan_step, totals, (kv_blocks, domain_blocks, firsts))]
    add x16 -> x0, other arithmetic: 10.3 us -> none  [block_place(): return looked_up * group_rows + storage % group_rows]
    select_n x17 -> x2, other arithmetic: 10.3 us -> 0.02 us  [block_place(): block_index = storage // group_rows]
  transfers between devices with their start and end apart: 6 -> 6, of which waited for: 5 -> 6; matrix products, arithmetic and copies ran while one was open for 41% -> 7% of each run, Pallas kernels for 0% -> 10%
where the time goes in v1:
time: 551 us; the launch traced here: 548 us
  waiting for transfers between devices  410 us (74%)
  Pallas kernels  53.4 us (10%)
  matrix products  38.4 us (7%)
  blocking collectives  17 us (3%)
  between operations  13.6 us (2%)
  other arithmetic  8.86 us (2%)
  local copies, waits for them, and re-layouts  6.62 us (1%)
    all_gather x1, waiting for transfers between devices, shards(): kv_all = lax.all_gather(keyvals, ('ctx', 'row'), axis=0, tiled=True)  113 us
    all_gather x1, waiting for transfers between devices, shards(): lax.all_gather(query_weight, 'row', axis=0, tiled=True)  73.3 us
    all_gather x1, waiting for transfers between devices, shards(): all_heads = lax.all_gather(attended, 'col', axis=1, tiled=True)  58.7 us
    all_gather x1, waiting for transfers between devices, shards(): lax.all_gather(pair_weight, 'row', axis=0, tiled=True)  56.3 us
    all_gather x1, waiting for transfers between devices, shards(): lax.all_gather(out_weight, 'row', axis=0, tiled=True)  54.2 us
    pallas_call x1, Pallas kernels, attention(): pl.pallas_call(attention_body, grid_spec=pltpu.PrefetchScalarGridSpec(num...  53.4 us
    all_gather x1, waiting for transfers between devices, shards(): whole = lax.all_gather(events, 'col', axis=1, tiled=True)  52.8 us
    all_gather x1, blocking collectives, shards(): domain_all = lax.all_gather(domain_ids, ('ctx', 'row'), axis=0, tiled=True)  17 us
  transfers between devices with their start and end apart: 6, of which 6 were waited for; matrix products, arithmetic and copies ran while one was open for 7% of the time, Pallas kernels for 10%

profile of v1, /device:TPU:27, one launch (start us, length us, event | category | flops | bytes accessed | tf_op | source)
XLA Modules:
  0.0 548.4 jit_solution(15648348979158407078)
XLA Ops:
  6.5 0.0 all-gather.8.cloned.1.call-start
  6.5 0.7 all-gather.8.cloned.1.call-update
  7.3 0.0 all-gather.12.cloned.1.call-start
  7.3 3.0 constant_dynamic-slice_fusion
  10.4 2.7 reshape.159
  13.1 0.0 all-gather.12.cloned.1.call-update
  13.1 0.0 all-gather.10.cloned.1.call-start
  13.1 0.7 all-gather.10.cloned.1.call-update
  13.8 0.0 all-gather.14.cloned.1.call-start
  13.9 52.8 %all-gather.8.cloned.1.call-done = bf16[512,4096]{1,0:T(8,128)(2,1)} async-done(((bf16[512,2048]{1,0:T(8,128)(2,1)}), bf16[512,4096]{1,0:T(8,128)(2,1)}) %all-gather.8.cloned.1.call-update) | async-done | bytes 4194320 | tf_op jit(solution)/shard_map/all_gather | solution.py:119
  66.6 3.1 fusion
  69.7 56.3 %all-gather.12.cloned.1.call-done = bf16[4096,1024]{1,0:T(8,128)(2,1)} async-done(((bf16[1024,1024]{1,0:T(8,128)(2,1)}), bf16[4096,1024]{1,0:T(8,128)(2,1)}) %all-gather.12.cloned.1.call-update) | async-done | bytes 8388624 | tf_op jit(solution)/shard_map/all_gather | solution.py:130
  126.0 10.2 %fusion.5 = bf16[512,1024]{1,0:T(8,128)(2,1)} fusion(bf16[4096,1024]{1,0:T(8,128)(2,1)} %all-gather.12.cloned.1.call-done, bf16[512,4096]{1,0:T(8,128)(2,1)} %all-gather.8.cloned.1.call-done, f32[512]{0:T(512)S(1)} %add_rsqrt_fusion), kind=kOutput, calls=%fused_computation.8 | convolution fusion | flops 4301783040 | bytes 13633536 | tf_op jit(solution)/shard_map/dot_general | solution.py:128
  136.2 0.0 copy-start.1
  136.2 0.0 copy-start.2
  136.2 0.0 copy-start
  136.2 0.0 all-gather.14.cloned.1.call-update
  136.2 0.0 all-gather.18.cloned.1.call-start
  136.3 0.5 all-gather.18.cloned.1.call-update
  136.8 0.0 all-gather.16.cloned.1.call-start
  136.9 0.0 copy-done.1
  136.9 0.1 select_reduce_fusion
  137.0 0.5 slice.4
  137.5 0.0 copy-done.2
  137.5 0.1 broadcast_in_dim.94
  137.6 0.1 broadcast_in_dim.91
  137.7 0.1 copy.12
  137.9 0.0 copy-done
  137.9 17.0 %all-gather = s32[16,1,512]{2,1,0:T(1,128)S(1)} all-gather(s32[1,1,512]{2,1,0:T(1,128)S(1)} %bitcast.9), channel_id=1, replica_groups=mesh['ctx'=4,'row'=4,'col'=2] {'ctx','row'}, dimensions={0}, use_global_device_ids=true | all-gather | bytes 34816 | tf_op jit(solution)/shard_map/all_gather | solution.py:152
  154.9 0.1 select_reduce_fusion.1
  155.0 0.7 compare_select_fusion.3.kind_ref
  155.7 0.1 select_select_fusion.bias_ref
  155.8 0.1 and_convert_fusion.1.qhot_ref
  155.9 4.7 and_convert_fusion.khot_ref
  160.6 73.3 %all-gather.10.cloned.1.call-done = bf16[4096,2048]{1,0:T(8,128)(2,1)} async-done(((bf16[1024,2048]{1,0:T(8,128)(2,1)}), bf16[4096,2048]{1,0:T(8,128)(2,1)}) %all-gather.10.cloned.1.call-update) | async-done | bytes 16777232 | tf_op jit(solution)/shard_map/all_gather | solution.py:135
  233.9 13.7 %multiply_convert_fusion.q_ref = bf16[512,2048]{1,0:T(8,128)(2,1)S(1)} fusion(bf16[4096,2048]{1,0:T(8,128)(2,1)} %all-gather.10.cloned.1.call-done, bf16[512,4096]{1,0:T(8,128)(2,1)} %all-gather.8.cloned.1.call-done, f32[512]{0:T(512)S(1)} %add_rsqrt_fusion), kind=kOutput, calls=%fused_computation.4 | convolution fusion | flops 8598323200 | bytes 23070720 | tf_op jit(solution)/shard_map/dot_general | solution.py:133
  247.5 113.3 %all-gather.14.cloned.1.call-done.kv_ref = bf16[8192,1024]{1,0:T(8,128)(2,1)} async-done(((bf16[512,1024]{1,0:T(8,128)(2,1)}), bf16[8192,1024]{1,0:T(8,128)(2,1)}) %all-gather.14.cloned.1.call-update) | async-done | bytes 16777232 | tf_op jit(solution)/shard_map/all_gather | solution.py:151
  360.8 53.4 %shard_map.73 = bf16[512,2048]{1,0:T(8,128)(2,1)} custom-call(s32[16]{0:T(128)S(1)} %compare_select_fusion.3.kind_ref, bf16[512,2048]{1,0:T(8,128)(2,1)S(1)} %multiply_convert_fusion.q_ref, bf16[8192,1024]{1,0:T(8,128)(2,1)} %all-gather.14.cloned.1.call-done.kv_ref, bf16[512,128]{1,0:T(8,128)(2,1)S(1)} %and_convert_fusion.1.qhot_ref, ...), custom_call_target="tpu_custom_call" | custom-call | flops 34359738368 | bytes 16777216 | tf_op jit(solution)/shard_map/pallas_call | solution.py:76
  414.2 0.0 all-gather.16.cloned.1.call-update
  414.2 54.2 %all-gather.18.cloned.1.call-done = bf16[4096,2048]{1,0:T(8,128)(2,1)} async-done(((bf16[1024,2048]{1,0:T(8,128)(2,1)}), bf16[4096,2048]{1,0:T(8,128)(2,1)}) %all-gather.18.cloned.1.call-update) | async-done | bytes 16777232 | tf_op jit(solution)/shard_map/all_gather | solution.py:166
  468.3 58.7 %all-gather.16.cloned.1.call-done = bf16[512,4096]{1,0:T(8,128)(2,1)} async-done(((bf16[512,2048]{1,0:T(8,128)(2,1)}), bf16[512,4096]{1,0:T(8,128)(2,1)}) %all-gather.16.cloned.1.call-update) | async-done | bytes 4194320 | tf_op jit(solution)/shard_map/all_gather | solution.py:163
  527.0 14.5 %convolution_convert_fusion = bf16[512,2048]{1,0:T(8,128)(2,1)} fusion(bf16[512,4096]{1,0:T(8,128)(2,1)} %all-gather.16.cloned.1.call-done, bf16[4096,2048]{1,0:T(8,128)(2,1)} %all-gather.18.cloned.1.call-done), kind=kOutput, calls=%fused_computation.6 | convolution fusion | flops 8590983168 | bytes 23068672 | tf_op jit(solution)/shard_map/dot_general | solution.py:164
  (9 shorter events, 0.1 us)
Async XLA Ops:
  6.5 60.1 %all-gather.8.cloned.1.call-start = ((), (), s32[]{:S(2)}) async-start(), calls=%async_computation | async-start | bytes 6291456 | tf_op jit(solution)/shard_map/all_gather | solution.py:119
  7.3 118.8 %all-gather.12.cloned.1.call-start = ((), (), s32[]{:S(2)}) async-start(), calls=%async_computation.2 | async-start | bytes 10485760 | tf_op jit(solution)/shard_map/all_gather | solution.py:130
  13.1 220.8 %all-gather.10.cloned.1.call-start = ((), (), s32[]{:S(2)}) async-start(), calls=%async_computation.1 | async-start | bytes 20971520 | tf_op jit(solution)/shard_map/all_gather | solution.py:135
  13.8 347.0 %all-gather.14.cloned.1.call-start = ((), (), s32[]{:S(2)}) async-start(), calls=%async_computation.3 | async-start | bytes 17825792 | tf_op jit(solution)/shard_map/all_gather | solution.py:151
  136.2 0.7 copy-start.1
  136.2 1.3 copy-start.2
  136.2 1.7 copy-start
  136.2 332.1 %all-gather.18.cloned.1.call-start = ((), (), s32[]{:S(2)}) async-start(), calls=%async_computation.5 | async-start | bytes 20971520 | tf_op jit(solution)/shard_map/all_gather | solution.py:166
  136.8 390.2 %all-gather.16.cloned.1.call-start = ((), (), s32[]{:S(2)}) async-start(), calls=%async_computation.4 | async-start | bytes 6291456 | tf_op jit(solution)/shard_map/all_gather | solution.py:163
Sparse Core Ops, SparseCore 0:
  8.9 57.6 all-gather.7
  68.2 57.7 all-gather.11
  127.6 106.2 all-gather.9
  235.9 124.8 all-gather.13
  362.2 106.1 all-gather.17
  469.7 57.2 all-gather.15

commit v2 on v1

--- a/solution.py
+++ b/solution.py
@@ -102,6 +102,222 @@
     )(kinds, queries, kv_all, query_hot, key_hot, bias_lanes, inv_count)
 
 
+MESH = pl.DeviceIdType.MESH
+CHUNKS = 4
+
+
+def partner(index):
+    return index + 1 - 2 * (index % 2)
+
+
+def weights_body(col_count, n_weights, *refs):
+    events = refs[0]
+    shards_in = refs[1:1 + n_weights]
+    wide = refs[1 + n_weights]
+    gathered = refs[2 + n_weights:2 + 2 * n_weights]
+    (local_sem, ev_send, ev_recv, x_send, x_recv, z_send, z_recv, o_send, o_recv,
+     f_send, f_recv, g_send, g_recv) = refs[2 + 2 * n_weights:]
+    z, r, c = lax.axis_index("ctx"), lax.axis_index("row"), lax.axis_index("col")
+    mate = {"row": partner(r)}
+    across = {"row": (r + 2) % 4}
+    beside = {"ctx": partner(z)}
+    far = (r + 2) % 4
+    mine, other = z % 2, 1 - z % 2
+
+    barrier = pltpu.get_barrier_semaphore()
+    peers = [{"col": (c + k) % col_count} for k in range(1, col_count)]
+    for peer in [mate, across, beside] + peers:
+        pl.semaphore_signal(barrier, inc=1, device_id=peer, device_id_type=MESH)
+    pl.semaphore_wait(barrier, 3 + len(peers))
+
+    def remote(src, dst, send, recv, target):
+        return pltpu.make_async_remote_copy(
+            src_ref=src, dst_ref=dst, send_sem=send, recv_sem=recv,
+            device_id=target, device_id_type=MESH,
+        )
+
+    width = events.shape[1]
+    columns = pl.ds(pl.multiple_of(c * width, 128), width)
+    spread = [
+        remote(events, wide.at[:, columns], ev_send.at[k], ev_recv.at[k], peer)
+        for k, peer in enumerate(peers)
+    ]
+
+    def piece(w, half, i):
+        size = shards_in[w].shape[0] // (2 * CHUNKS)
+        return pl.ds(pl.multiple_of((half * CHUNKS + i) * size, 16), size)
+
+    steps = [(w, i) for w in range(n_weights) for i in range(CHUNKS)]
+    cross, relay, over, over_late = [], [], [], []
+    for n, (w, i) in enumerate(steps):
+        rows, late = piece(w, mine, i), piece(w, other, i)
+        out = gathered[w]
+        cross.append(remote(
+            shards_in[w].at[rows], out.at[r, rows], x_send.at[n], x_recv.at[n], across))
+        relay.append(remote(
+            out.at[far, rows], out.at[far, rows], z_send.at[n], z_recv.at[n], beside))
+        over.append(remote(
+            out.at[far, rows], out.at[far, rows], f_send.at[n], f_recv.at[n], mate))
+        over_late.append(remote(
+            out.at[far, late], out.at[far, late], g_send.at[n], g_recv.at[n], mate))
+    own = [
+        remote(shards_in[w], gathered[w].at[r], o_send.at[w], o_recv.at[w], mate)
+        for w in range(n_weights)
+    ]
+    keep = [pltpu.make_async_copy(events, wide.at[:, columns], local_sem.at[n_weights])] + [
+        pltpu.make_async_copy(shards_in[w], gathered[w].at[r], local_sem.at[w])
+        for w in range(n_weights)
+    ]
+    for copy in cross + spread + own + keep:
+        copy.start()
+    for n in range(len(steps)):
+        cross[n].wait_recv()
+        relay[n].start()
+        over[n].start()
+        if n >= 1:
+            relay[n - 1].wait_recv()
+            over_late[n - 1].start()
+    relay[-1].wait_recv()
+    over_late[-1].start()
+    for copy in over + over_late + own + spread:
+        copy.wait_recv()
+    for copy in cross + relay + over + over_late + own + spread:
+        copy.wait_send()
+    for copy in keep:
+        copy.wait()
+
+
+def gather_weights(col_count, events, weights, name):
+    n = len(weights)
+    steps = n * CHUNKS
+    anywhere = pl.BlockSpec(memory_space=pl.ANY)
+    dma = pltpu.SemaphoreType.DMA
+    peers = max(1, col_count - 1)
+    return pl.pallas_call(
+        functools.partial(weights_body, col_count, n),
+        out_shape=[jax.ShapeDtypeStruct((events.shape[0], events.shape[1] * col_count), events.dtype)]
+        + [jax.ShapeDtypeStruct((4,) + w.shape, w.dtype) for w in weights],
+        in_specs=[anywhere] * (1 + n),
+        out_specs=[anywhere] * (1 + n),
+        scratch_shapes=[dma((n + 1,)), dma((peers,)), dma((peers,)), dma((steps,)), dma((steps,)),
+                        dma((steps,)), dma((steps,)), dma((n,)), dma((n,)),
+                        dma((steps,)), dma((steps,)), dma((steps,)), dma((steps,))],
+        compiler_params=pltpu.CompilerParams(collective_id=name, has_side_effects=True),
+    )(events, *weights)
+
+
+def spread_body(ctx_count, kv, dom, kv_all, dom_all, local_sem,
+                up_send, down_send, x_send, c_send, recv_sem):
+    z, r = lax.axis_index("ctx"), lax.axis_index("row")
+    far, near = (r + 2) % 4, partner(r)
+    barrier = pltpu.get_barrier_semaphore()
+
+    def greet(target):
+        pl.semaphore_signal(barrier, inc=1, device_id=target, device_id_type=MESH)
+
+    above, below = z < ctx_count - 1, z > 0
+    greet({"row": near})
+    greet({"row": far})
+    pl.when(above)(lambda: greet({"ctx": z + 1}))
+    pl.when(below)(lambda: greet({"ctx": z - 1}))
+    pl.semaphore_wait(barrier, 2 + (z + ctx_count - 1) // ctx_count + (2 * ctx_count - 2 - z) // ctx_count)
+
+    def copies(zz, rr, send, target, first=False):
+        pair = []
+        for k, (src, dst) in enumerate(((kv, kv_all), (dom, dom_all))):
+            pair.append(pltpu.make_async_remote_copy(
+                src_ref=src if first else dst.at[zz, rr], dst_ref=dst.at[zz, rr],
+                send_sem=send.at[zz, rr, k] if send is x_send or send is c_send else send.at[zz, k],
+                recv_sem=recv_sem.at[zz, rr, k], device_id=target, device_id_type=MESH))
+        return pair
+
+    def start(pair):
+        for copy in pair:
+            copy.start()
+
+    def sent(pair):
+        for copy in pair:
+            copy.wait_send()
+
+    def landed(zz, rr):
+        for copy in copies(zz, rr, x_send, {"row": far}):
+            copy.wait_recv()
+
+    keep = [pltpu.make_async_copy(kv, kv_all.at[z, r], local_sem.at[0]),
+            pltpu.make_async_copy(dom, dom_all.at[z, r], local_sem.at[1])]
+
+    def up(zz, first=False):
+        return copies(zz, r, up_send, {"ctx": z + 1}, first)
+
+    def down(zz, first=False):
+        return copies(zz, r, down_send, {"ctx": z - 1}, first)
+
+    def to_far(zz, first=False):
+        return copies(zz, r, x_send, {"row": far}, first)
+
+    def to_near(zz, rr, first=False):
+        return copies(zz, rr, c_send, {"row": near}, first)
+
+    pl.when(above)(lambda: start(up(z, True)))
+    pl.when(below)(lambda: start(down(z, True)))
+    start(to_far(z, True))
+    start(to_near(z, r, True))
+    for copy in keep:
+        copy.start()
+    landed(z, far)
+    start(to_near(z, far))
+    for d in range(1, ctx_count):
+        @pl.when(z >= d)
+        def _():
+            landed(z - d, r)
+            pl.when(above)(lambda: start(up(z - d)))
+            start(to_far(z - d))
+            start(to_near(z - d, r))
+
+        @pl.when(z + d < ctx_count)
+        def _():
+            landed(z + d, r)
+            pl.when(below)(lambda: start(down(z + d)))
+            start(to_far(z + d))
+            start(to_near(z + d, r))
+
+        @pl.when(z >= d)
+        def _():
+            landed(z - d, far)
+            start(to_near(z - d, far))
+
+        @pl.when(z + d < ctx_count)
+        def _():
+            landed(z + d, far)
+            start(to_near(z + d, far))
+    mate_far = (near + 2) % 4
+    for zz in range(ctx_count):
+        landed(zz, near)
+        landed(zz, mate_far)
+        sent(to_far(zz))
+        sent(to_near(zz, r))
+        sent(to_near(zz, far))
+        pl.when(above & (z >= zz))(lambda zz=zz: sent(up(zz)))
+        pl.when(below & (z <= zz))(lambda zz=zz: sent(down(zz)))
+    for copy in keep:
+        copy.wait()
+
+
+def gather_keyvals(ctx_count, keyvals, domains, name):
+    anywhere = pl.BlockSpec(memory_space=pl.ANY)
+    dma = pltpu.SemaphoreType.DMA
+    return pl.pallas_call(
+        functools.partial(spread_body, ctx_count),
+        out_shape=[jax.ShapeDtypeStruct((ctx_count, 4) + keyvals.shape, keyvals.dtype),
+                   jax.ShapeDtypeStruct((ctx_count, 4) + domains.shape, domains.dtype)],
+        in_specs=[anywhere] * 2,
+        out_specs=[anywhere] * 2,
+        scratch_shapes=[dma((2,)), dma((ctx_count, 2)), dma((ctx_count, 2)), dma((ctx_count, 4, 2)),
+                        dma((ctx_count, 4, 2)), dma((ctx_count, 4, 2))],
+        compiler_params=pltpu.CompilerParams(collective_id=name, has_side_effects=True),
+    )(keyvals, domains)
+
+
 def hot_lanes(domains):
     lane = lax.broadcasted_iota(jnp.int32, (1, LANES), 1)
     return ((lane % HALF == domains[:, None]) & (lane < 2 * HALF)).astype(jnp.bfloat16)
@@ -116,23 +332,26 @@
     rows_axis = lax.axis_size("row")
     group_rows = row_count * rows_axis
     scale_factor = 1.0 / math.sqrt(HD)
-    whole = lax.all_gather(events, "col", axis=1, tiled=True)
+    col_count = lax.axis_size("col")
+    pair_start = lax.axis_index("col") * head_count // group_size
+    pair_weight = lax.dynamic_slice_in_dim(keyval_weight, pair_start, pair_heads, 1)
+    pair_weight = pair_weight.reshape(keyval_weight.shape[0], pair_heads * 2 * HD)
+    whole, pair_all, query_all = gather_weights(col_count, events, (pair_weight, query_weight), 1)
+    pair_all = pair_all.reshape(-1, pair_all.shape[-1])
+    query_all = query_all.reshape(-1, query_all.shape[-1])
     wide_events = whole.astype(jnp.float32)
     normed = (
         wide_events
         * lax.rsqrt(jnp.mean(wide_events * wide_events, axis=1, keepdims=True) + norm_eps)
     ).astype(jnp.bfloat16)
-    pair_start = lax.axis_index("col") * head_count // group_size
-    pair_weight = lax.dynamic_slice_in_dim(keyval_weight, pair_start, pair_heads, 1)
-    pair_weight = pair_weight.reshape(keyval_weight.shape[0], pair_heads * 2 * HD)
     pair_sums = jnp.dot(
         normed,
-        lax.all_gather(pair_weight, "row", axis=0, tiled=True),
+        pair_all,
         preferred_element_type=jnp.float32,
     )
     query_sums = jnp.dot(
         normed,
-        lax.all_gather(query_weight, "row", axis=0, tiled=True),
+        query_all,
         preferred_element_type=jnp.float32,
     )
     queries = (query_sums * (0.5 * scale_factor)).astype(jnp.bfloat16)
@@ -148,8 +367,11 @@
     lane = jnp.arange(LANES, dtype=jnp.int32)[None, :]
     bias_lanes = jnp.where(lane < HALF, high[:, None], jnp.where(lane < 2 * HALF, low[:, None], 0.0))
     bias_lanes = bias_lanes.reshape(pair_heads, group_heads, LANES)
-    kv_all = lax.all_gather(keyvals, ("ctx", "row"), axis=0, tiled=True)
-    domain_all = lax.all_gather(domain_ids, ("ctx", "row"), axis=0, tiled=True)
+    kv_all, domain_all = gather_keyvals(
+        lax.axis_size("ctx"), keyvals, domain_ids.reshape(-1, 128), 2
+    )
+    kv_all = kv_all.reshape(-1, kv_all.shape[-1])
+    domain_all = domain_all.reshape(-1)
     tiles = kv_all.shape[0] // row_count
     tile_first = block_place(
         row_count * jnp.arange(tiles, dtype=jnp.int32), group_rows, block_order

time: 551 us -> 694 us (1.26); the launches traced: 548 us -> 684 us
  Pallas kernels: 53.4 us -> 430 us
  waiting for transfers between devices: 410 us -> 190 us
  blocking collectives: 17 us -> 0 us
    pallas_call x0 -> x2, Pallas kernels: none -> 377 us  [the longest x1 257 us: gather_weights(): pl.pallas_call(functools.partial(weights_body, col_count, n), out_shape=[...]
    all_gather x4 -> x0, waiting for transfers between devices: 296 us -> none  [the longest x1 113 us: shards(): kv_all = lax.all_gather(keyvals, ('ctx', 'row'), axis=0, tiled=True)]
    all_gather x1, waiting for transfers between devices: 54.2 us -> 107 us  [shards(): lax.all_gather(out_weight, 'row', axis=0, tiled=True)]
    all_gather x1, waiting for transfers between devices: 58.7 us -> 82.1 us  [shards(): all_heads = lax.all_gather(attended, 'col', axis=1, tiled=True)]
    all_gather x1 -> x0, blocking collectives: 17 us -> none  [shards(): domain_all = lax.all_gather(domain_ids, ('ctx', 'row'), axis=0, tiled=True)]
  transfers between devices with their start and end apart: 6 -> 2, of which waited for: 6 -> 2; matrix products, arithmetic and copies ran while one was open for 7% -> 0% of each run, Pallas kernels for 10% -> 0%
where the time goes in v2:
time: 694 us; the launch traced here: 684 us
  Pallas kernels  430 us (62%)
  waiting for transfers between devices  190 us (27%)
  matrix products  33 us (5%)
  between operations  13.6 us (2%)
  other arithmetic  10.8 us (2%)
    pallas_call x1, Pallas kernels, gather_weights(): pl.pallas_call(functools.partial(weights_body, col_count, n), out_shape=[...  257 us
    pallas_call x1, Pallas kernels, gather_keyvals(): pl.pallas_call(functools.partial(spread_body, ctx_count), out_shape=[jax....  120 us
    all_gather x1, waiting for transfers between devices, shards(): lax.all_gather(out_weight, 'row', axis=0, tiled=True)  107 us
    all_gather x1, waiting for transfers between devices, shards(): all_heads = lax.all_gather(attended, 'col', axis=1, tiled=True)  82.1 us
    pallas_call x1, Pallas kernels, attention(): pl.pallas_call(attention_body, grid_spec=pltpu.PrefetchScalarGridSpec(num...  52.9 us
    dot_general x1, matrix products, shards(): jnp.dot(all_heads, lax.all_gather(out_weight, 'row', axis=0, tiled=True),...  14.5 us
  transfers between devices with their start and end apart: 2, of which 2 were waited for; matrix products, arithmetic and copies ran while one was open for 0% of the time, Pallas kernels for 0%

profile of v2, /device:TPU:27, one launch (start us, length us, event | category | flops | bytes accessed | tf_op | source)
XLA Modules:
  0.0 683.8 jit_solution(4929560470001279130)
XLA Ops:
  6.5 0.0 all-gather.3.cloned.1.call-start
  6.6 0.7 select_reduce_fusion.1
  7.3 0.7 select_reduce_fusion
  8.1 0.5 slice.4
  8.6 3.0 constant_dynamic-slice_fusion
  11.6 2.7 reshape.171.refs_1_
  14.3 257.1 %shard_map.73 = (bf16[512,4096]{1,0:T(8,128)(2,1)}, bf16[4,1024,1024]{2,1,0:T(8,128)(2,1)}, bf16[4,1024,2048]{2,1,0:T(8,128)(2,1)}) custom-call(bf16[512,2048]{1,0:T(8,128)(2,1)} %refs_0_.1, bf16[1024,1024]{1,0:T(8,128)(2,1)} %reshape.171.refs_1_, bf16[1024,2048]{1,0:T(8,128)(2,1)} %refs_2_.1), custom_call_target="tpu_custom_call" | custom-call | tf_op jit(solution)/shard_map/pallas_call | solution.py:196
  271.4 0.0 copy-start
  271.4 0.0 slice-start
  271.5 3.2 fusion
  274.7 0.2 copy-done
  274.9 0.0 slice-start.1
  274.9 12.9 %multiply_convert_fusion.q_ref = bf16[512,2048]{1,0:T(8,128)(2,1)S(1)} fusion(bf16[4096,2048]{1,0:T(8,128)(2,1)} %bitcast.15, bf16[512,4096]{1,0:T(8,128)(2,1)S(1)} %copy-done, f32[512]{0:T(512)S(1)} %add_rsqrt_fusion), kind=kOutput, calls=%fused_computation.4 | convolution fusion | flops 8598323200 | bytes 23070720 | tf_op jit(solution)/shard_map/dot_general | solution.py:352
  287.8 0.0 slice-done
  287.8 0.0 slice-done.1
  287.8 0.0 copy-start.1
  287.8 0.0 copy-start.2
  287.9 5.5 fusion.5.kv
  293.4 119.7 %shard_map.74 = (bf16[4,4,512,1024]{3,2,1,0:T(8,128)(2,1)}, s32[4,4,4,128]{3,2,1,0:T(4,128)}) custom-call(bf16[512,1024]{1,0:T(8,128)(2,1)} %fusion.5.kv, s32[4,128]{1,0:T(4,128)} %bitcast.12), custom_call_target="tpu_custom_call" | custom-call | tf_op jit(solution)/shard_map/pallas_call | solution.py:309
  413.1 0.0 copy-done.1
  413.2 0.1 and_convert_fusion.1.qhot_ref
  413.3 5.2 and_convert_fusion.khot_ref
  418.5 0.0 copy-done.2
  418.5 0.1 broadcast_in_dim.93
  418.6 0.1 broadcast_in_dim.90
  418.7 0.1 copy.11
  418.9 0.6 compare_select_fusion.3.kind_ref
  419.5 0.1 select_select_fusion.bias_ref
  419.5 52.9 %shard_map.75 = bf16[512,2048]{1,0:T(8,128)(2,1)} custom-call(s32[16]{0:T(128)S(1)} %compare_select_fusion.3.kind_ref, bf16[512,2048]{1,0:T(8,128)(2,1)S(1)} %multiply_convert_fusion.q_ref, bf16[8192,1024]{1,0:T(8,128)(2,1)} %bitcast.14, bf16[512,128]{1,0:T(8,128)(2,1)S(1)} %and_convert_fusion.1.qhot_ref, bf16[8192,128]{1,0:T(8,128)(2,1)} %and_convert_fusion.khot_ref, ...), custom_call_target="tpu_custom_call" | custom-call | flops 34359738368 | bytes 16777216 | tf_op jit(solution)/shard_map/pallas_call | solution.py:76
  472.5 0.0 all-gather.3.cloned.1.call-update
  472.5 0.0 all-gather.5.cloned.1.call-start
  472.5 0.7 all-gather.5.cloned.1.call-update
  473.2 82.1 %all-gather.3.cloned.1.call-done = bf16[512,4096]{1,0:T(8,128)(2,1)} async-done(((bf16[512,2048]{1,0:T(8,128)(2,1)}), bf16[512,4096]{1,0:T(8,128)(2,1)}) %all-gather.3.cloned.1.call-update) | async-done | bytes 4194320 | tf_op jit(solution)/shard_map/all_gather | solution.py:385
  555.4 107.0 %all-gather.5.cloned.1.call-done = bf16[4096,2048]{1,0:T(8,128)(2,1)} async-done(((bf16[1024,2048]{1,0:T(8,128)(2,1)}), bf16[4096,2048]{1,0:T(8,128)(2,1)}) %all-gather.5.cloned.1.call-update) | async-done | bytes 16777232 | tf_op jit(solution)/shard_map/all_gather | solution.py:388
  662.4 14.5 %convolution_convert_fusion = bf16[512,2048]{1,0:T(8,128)(2,1)} fusion(bf16[512,4096]{1,0:T(8,128)(2,1)} %all-gather.3.cloned.1.call-done, bf16[4096,2048]{1,0:T(8,128)(2,1)} %all-gather.5.cloned.1.call-done), kind=kOutput, calls=%fused_computation.6 | convolution fusion | flops 8590983168 | bytes 23068672 | tf_op jit(solution)/shard_map/dot_general | solution.py:386
  (10 shorter events, 0.1 us)
Async XLA Ops:
  6.5 548.8 %all-gather.3.cloned.1.call-start = ((), (), s32[]{:S(2)}) async-start(), calls=%async_computation | async-start | bytes 6291456 | tf_op jit(solution)/shard_map/all_gather | solution.py:385
  271.4 3.5 copy-start
  271.4 16.4 %slice-start = ((s8[8388608]{0:T(1024)(128)(4,1)}), s8[4194304]{0:T(1024)(128)(4,1)S(1)}, s32[]{:S(2)}) async-start(s8[8388608]{0:T(1024)(128)(4,1)} %bitcast.16), calls=%async_computation.2 | async-start | bytes 8388608
  274.9 12.9 %slice-start.1 = ((s8[8388608]{0:T(1024)(128)(4,1)}), s8[4194304]{0:T(1024)(128)(4,1)S(1)}, s32[]{:S(2)}) async-start(s8[8388608]{0:T(1024)(128)(4,1)} %bitcast.16), calls=%async_computation.3 | async-start | bytes 8388608
  287.8 125.3 %copy-start.1 = (s32[512]{0:T(512)S(1)}, s32[512]{0:T(512)}, u32[]{:S(2)}) copy-start(s32[512]{0:T(512)} %param.8) | copy-start | bytes 6148
  287.8 130.7 %copy-start.2 = (f32[16]{0:T(128)S(1)}, f32[16]{0:T(128)}, u32[]{:S(2)}) copy-start(f32[16]{0:T(128)} %param.12) | copy-start | bytes 196
  472.5 189.9 %all-gather.5.cloned.1.call-start = ((), (), s32[]{:S(2)}) async-start(), calls=%async_computation.1 | async-start | bytes 20971520 | tf_op jit(solution)/shard_map/all_gather | solution.py:388
Sparse Core Ops, SparseCore 0:
  472.6 82.6 all-gather.2
  556.9 105.4 all-gather.4

commit v3 on v2

--- a/solution.py
+++ b/solution.py
@@ -110,100 +110,46 @@
     return index + 1 - 2 * (index % 2)
 
 
-def weights_body(col_count, n_weights, *refs):
-    events = refs[0]
-    shards_in = refs[1:1 + n_weights]
-    wide = refs[1 + n_weights]
-    gathered = refs[2 + n_weights:2 + 2 * n_weights]
-    (local_sem, ev_send, ev_recv, x_send, x_recv, z_send, z_recv, o_send, o_recv,
-     f_send, f_recv, g_send, g_recv) = refs[2 + 2 * n_weights:]
-    z, r, c = lax.axis_index("ctx"), lax.axis_index("row"), lax.axis_index("col")
-    mate = {"row": partner(r)}
-    across = {"row": (r + 2) % 4}
-    beside = {"ctx": partner(z)}
-    far = (r + 2) % 4
-    mine, other = z % 2, 1 - z % 2
-
+def columns_body(col_count, part, wide, local_sem, send, recv):
+    c = lax.axis_index("col")
+    peers = [{"col": (c + k) % col_count} for k in range(1, col_count)]
     barrier = pltpu.get_barrier_semaphore()
-    peers = [{"col": (c + k) % col_count} for k in range(1, col_count)]
-    for peer in [mate, across, beside] + peers:
+    for peer in peers:
         pl.semaphore_signal(barrier, inc=1, device_id=peer, device_id_type=MESH)
-    pl.semaphore_wait(barrier, 3 + len(peers))
-
-    def remote(src, dst, send, recv, target):
-        return pltpu.make_async_remote_copy(
-            src_ref=src, dst_ref=dst, send_sem=send, recv_sem=recv,
-            device_id=target, device_id_type=MESH,
-        )
-
-    width = events.shape[1]
+    pl.semaphore_wait(barrier, len(peers))
+    width = part.shape[1]
+    size = part.shape[0] // CHUNKS
     columns = pl.ds(pl.multiple_of(c * width, 128), width)
-    spread = [
-        remote(events, wide.at[:, columns], ev_send.at[k], ev_recv.at[k], peer)
-        for k, peer in enumerate(peers)
-    ]
-
-    def piece(w, half, i):
-        size = shards_in[w].shape[0] // (2 * CHUNKS)
-        return pl.ds(pl.multiple_of((half * CHUNKS + i) * size, 16), size)
-
-    steps = [(w, i) for w in range(n_weights) for i in range(CHUNKS)]
-    cross, relay, over, over_late = [], [], [], []
-    for n, (w, i) in enumerate(steps):
-        rows, late = piece(w, mine, i), piece(w, other, i)
-        out = gathered[w]
-        cross.append(remote(
-            shards_in[w].at[rows], out.at[r, rows], x_send.at[n], x_recv.at[n], across))
-        relay.append(remote(
-            out.at[far, rows], out.at[far, rows], z_send.at[n], z_recv.at[n], beside))
-        over.append(remote(
-            out.at[far, rows], out.at[far, rows], f_send.at[n], f_recv.at[n], mate))
-        over_late.append(remote(
-            out.at[far, late], out.at[far, late], g_send.at[n], g_recv.at[n], mate))
-    own = [
-        remote(shards_in[w], gathered[w].at[r], o_send.at[w], o_recv.at[w], mate)
-        for w in range(n_weights)
-    ]
-    keep = [pltpu.make_async_copy(events, wide.at[:, columns], local_sem.at[n_weights])] + [
-        pltpu.make_async_copy(shards_in[w], gathered[w].at[r], local_sem.at[w])
-        for w in range(n_weights)
-    ]
-    for copy in cross + spread + own + keep:
+    copies = []
+    for i in range(CHUNKS):
+        rows = pl.ds(i * size, size)
+        for k, peer in enumerate(peers):
+            copies.append(pltpu.make_async_remote_copy(
+                src_ref=part.at[rows], dst_ref=wide.at[rows, columns],
+                send_sem=send.at[k, i], recv_sem=recv.at[k, i],
+                device_id=peer, device_id_type=MESH))
+    keep = pltpu.make_async_copy(part, wide.at[:, columns], local_sem)
+    for copy in copies:
         copy.start()
-    for n in range(len(steps)):
-        cross[n].wait_recv()
-        relay[n].start()
-        over[n].start()
-        if n >= 1:
-            relay[n - 1].wait_recv()
-            over_late[n - 1].start()
-    relay[-1].wait_recv()
-    over_late[-1].start()
-    for copy in over + over_late + own + spread:
-        copy.wait_recv()
-    for copy in cross + relay + over + over_late + own + spread:
-        copy.wait_send()
-    for copy in keep:
+    keep.start()
+    for copy in copies:
         copy.wait()
-
-
-def gather_weights(col_count, events, weights, name):
-    n = len(weights)
-    steps = n * CHUNKS
-    anywhere = pl.BlockSpec(memory_space=pl.ANY)
+    keep.wait()
+
+
+def gather_columns(col_count, part, name):
     dma = pltpu.SemaphoreType.DMA
-    peers = max(1, col_count - 1)
     return pl.pallas_call(
-        functools.partial(weights_body, col_count, n),
-        out_shape=[jax.ShapeDtypeStruct((events.shape[0], events.shape[1] * col_count), events.dtype)]
-        + [jax.ShapeDtypeStruct((4,) + w.shape, w.dtype) for w in weights],
-        in_specs=[anywhere] * (1 + n),
-        out_specs=[anywhere] * (1 + n),
-        scratch_shapes=[dma((n + 1,)), dma((peers,)), dma((peers,)), dma((steps,)), dma((steps,)),
-                        dma((steps,)), dma((steps,)), dma((n,)), dma((n,)),
-                        dma((steps,)), dma((steps,)), dma((steps,)), dma((steps,))],
-        compiler_params=pltpu.CompilerParams(collective_id=name, has_side_effects=True),
-    )(events, *weights)
+        functools.partial(columns_body, col_count),
+        out_shape=jax.ShapeDtypeStruct((part.shape[0], part.shape[1] * col_count), part.dtype),
+        in_specs=[pl.BlockSpec(memory_space=pltpu.VMEM)],
+        out_specs=pl.BlockSpec(memory_space=pl.ANY),
+        scratch_shapes=[dma, dma((col_count - 1, CHUNKS)), dma((col_count - 1, CHUNKS))],
+        compiler_params=pltpu.CompilerParams(
+            collective_id=name, has_side_effects=True, vmem_limit_bytes=16 * 1024 * 1024),
+        cost_estimate=pl.CostEstimate(
+            flops=0, bytes_accessed=32 * part.size * 2, transcendentals=0),
+    )(part)
 
 
 def spread_body(ctx_count, kv, dom, kv_all, dom_all, local_sem,
@@ -310,11 +256,14 @@
         functools.partial(spread_body, ctx_count),
         out_shape=[jax.ShapeDtypeStruct((ctx_count, 4) + keyvals.shape, keyvals.dtype),
                    jax.ShapeDtypeStruct((ctx_count, 4) + domains.shape, domains.dtype)],
-        in_specs=[anywhere] * 2,
+        in_specs=[pl.BlockSpec(memory_space=pltpu.VMEM)] * 2,
         out_specs=[anywhere] * 2,
         scratch_shapes=[dma((2,)), dma((ctx_count, 2)), dma((ctx_count, 2)), dma((ctx_count, 4, 2)),
                         dma((ctx_count, 4, 2)), dma((ctx_count, 4, 2))],
-        compiler_params=pltpu.CompilerParams(collective_id=name, has_side_effects=True),
+        compiler_params=pltpu.CompilerParams(collective_id=name, has_side_effects=True,
+                                             vmem_limit_bytes=16 * 1024 * 1024),
+        cost_estimate=pl.CostEstimate(
+            flops=0, bytes_accessed=128 * keyvals.size * 2, transcendentals=0),
     )(keyvals, domains)
 
 
@@ -336,9 +285,9 @@
     pair_start = lax.axis_index("col") * head_count // group_size
     pair_weight = lax.dynamic_slice_in_dim(keyval_weight, pair_start, pair_heads, 1)
     pair_weight = pair_weight.reshape(keyval_weight.shape[0], pair_heads * 2 * HD)
-    whole, pair_all, query_all = gather_weights(col_count, events, (pair_weight, query_weight), 1)
-    pair_all = pair_all.reshape(-1, pair_all.shape[-1])
-    query_all = query_all.reshape(-1, query_all.shape[-1])
+    pair_all = lax.all_gather(pair_weight, "row", axis=0, tiled=True)
+    query_all = lax.all_gather(query_weight, "row", axis=0, tiled=True)
+    whole = gather_columns(col_count, events, 1)
     wide_events = whole.astype(jnp.float32)
     normed = (
         wide_events
@@ -382,7 +331,7 @@
     attended = attention(
         kinds, queries, kv_all, hot_lanes(domain_ids), hot_lanes(domain_all), bias_lanes, inv_count
     )
-    all_heads = lax.all_gather(attended, "col", axis=1, tiled=True)
+    all_heads = gather_columns(col_count, attended, 3)
     out_sums = jnp.dot(
         all_heads,
         lax.all_gather(out_weight, "row", axis=0, tiled=True),

time: 694 us -> 455 us (0.66); the launches traced: 684 us -> 452 us
  waiting for transfers between devices: 190 us -> 4.83 us
  Pallas kernels: 430 us -> 369 us
  local copies, waits for them, and re-layouts: 6.78 us -> 16.4 us
    pallas_call x1 -> x2, Pallas kernels: 257 us -> 91.1 us  [gather_columns(): pl.pallas_call(functools.partial(columns_body, col_count), out_shape=jax....]
    all_gather x1, waiting for transfers between devices: 107 us -> 0.01 us  [shards(): lax.all_gather(out_weight, 'row', axis=0, tiled=True)]
    all_gather x1 -> x2, waiting for transfers between devices: 82.1 us -> 3.43 us  [the longest x1 3.43 us: shards(): pair_all = lax.all_gather(pair_weight, 'row', axis=0, tiled=True)]
    pallas_call x1, Pallas kernels: 120 us -> 186 us  [gather_keyvals(): pl.pallas_call(functools.partial(spread_body, ctx_count), out_shape=[jax....]
    pallas_call x1, Pallas kernels: 52.9 us -> 91.7 us  [attention(): pl.pallas_call(attention_body, grid_spec=pltpu.PrefetchScalarGridSpec(num...]
    unnamed x10 -> x14, local copies, waits for them, and re-layouts: 0.21 us -> 9.72 us
  transfers between devices with their start and end apart: 2 -> 3, of which waited for: 2 -> 1; matrix products, arithmetic and copies ran while one was open for 0% -> 8% of each run, Pallas kernels for 0% -> 82%
where the time goes in v3:
time: 455 us; the launch traced here: 452 us
  Pallas kernels  369 us (81%)
  matrix products  39.7 us (9%)
  local copies, waits for them, and re-layouts  16.4 us (4%)
  between operations  13.3 us (3%)
  other arithmetic  8.82 us (2%)
  waiting for transfers between devices  4.83 us (1%)
    pallas_call x1, Pallas kernels, gather_keyvals(): pl.pallas_call(functools.partial(spread_body, ctx_count), out_shape=[jax....  186 us
    pallas_call x1, Pallas kernels, attention(): pl.pallas_call(attention_body, grid_spec=pltpu.PrefetchScalarGridSpec(num...  91.7 us
    pallas_call x2, Pallas kernels, gather_columns(): pl.pallas_call(functools.partial(columns_body, col_count), out_shape=jax....  91.1 us
    dot_general x1, matrix products, shards(): query_sums = jnp.dot(normed, query_all, preferred_element_type=jnp.float32)  16 us
    dot_general x1, matrix products, shards(): jnp.dot(all_heads, lax.all_gather(out_weight, 'row', axis=0, tiled=True),...  14.5 us
    unnamed x14, local copies, waits for them, and re-layouts  9.72 us
    dot_general x1, matrix products, shards(): pair_sums = jnp.dot(normed, pair_all, preferred_element_type=jnp.float32)  9.18 us
  transfers between devices with their start and end apart: 3, of which 1 were waited for; matrix products, arithmetic and copies ran while one was open for 8% of the time, Pallas kernels for 82%

profile of v3, /device:TPU:27, one launch (start us, length us, event | category | flops | bytes accessed | tf_op | source)
XLA Modules:
  0.0 452.3 jit_solution(18331444646715244912)
XLA Ops:
  6.5 0.0 all-gather.6.cloned.1.call-start
  6.5 3.0 constant_dynamic-slice_fusion
  9.6 2.7 reshape.165
  12.3 0.0 all-gather.6.cloned.1.call-update
  12.3 0.0 copy-start.5
  12.3 0.0 copy-start.2
  12.3 0.0 all-gather.4.cloned.1.call-start
  12.4 0.7 all-gather.4.cloned.1.call-update
  13.1 0.0 all-gather.8.cloned.1.call-start
  13.1 0.7 all-gather.8.cloned.1.call-update
  13.8 0.0 copy-start.6
  13.8 0.0 copy-done.5
  13.9 0.1 select_reduce_fusion
  14.0 0.6 slice.4
  14.5 0.0 copy-done.2
  14.5 0.0 copy-start.3
  14.5 46.7 %shard_map.73 = bf16[512,4096]{1,0:T(8,128)(2,1)S(1)} custom-call(bf16[512,2048]{1,0:T(8,128)(2,1)S(1)} %copy-done.2), custom_call_target="tpu_custom_call" | custom-call | bytes 67108864 | tf_op jit(solution)/shard_map/pallas_call | solution.py:142
  61.2 0.0 copy-start
  61.2 2.0 copy-done
  63.3 0.0 copy-done.6
  63.3 0.1 broadcast_in_dim.93
  63.4 0.1 broadcast_in_dim.90
  63.5 0.1 copy.11
  63.7 0.1 select_reduce_fusion.1
  63.8 0.6 compare_select_fusion.3.kind_ref
  64.5 3.1 fusion
  67.5 0.1 select_select_fusion.bias_ref
  67.6 0.0 copy-done.3
  67.6 0.1 and_convert_fusion.1.qhot_ref
  67.8 3.4 all-gather.6.cloned.1.call-done
  71.2 9.2 %fusion.5.kv = bf16[512,1024]{1,0:T(8,128)(2,1)S(1)} fusion(bf16[4096,1024]{1,0:T(8,128)(2,1)} %all-gather.6.cloned.1.call-done, bf16[512,4096]{1,0:T(8,128)(2,1)} %copy-done, f32[512]{0:T(512)S(1)} %add_rsqrt_fusion), kind=kOutput, calls=%fused_computation.8 | convolution fusion | flops 4301783040 | bytes 13633536 | tf_op jit(solution)/shard_map/dot_general | solution.py:296
  80.4 186.3 %shard_map.74 = (bf16[4,4,512,1024]{3,2,1,0:T(8,128)(2,1)S(1)}, s32[4,4,4,128]{3,2,1,0:T(4,128)S(1)}) custom-call(bf16[512,1024]{1,0:T(8,128)(2,1)S(1)} %fusion.5.kv, s32[4,128]{1,0:T(4,128)S(1)} %bitcast.10), custom_call_target="tpu_custom_call" | custom-call | bytes 134217728 | tf_op jit(solution)/shard_map/pallas_call | solution.py:255
  266.7 0.0 copy-start.4
  266.7 5.7 %copy-done.4 = bf16[4,4,512,1024]{3,2,1,0:T(8,128)(2,1)} copy-done((bf16[4,4,512,1024]{3,2,1,0:T(8,128)(2,1)}, bf16[4,4,512,1024]{3,2,1,0:T(8,128)(2,1)S(1)}, u32[]{:S(2)}) %copy-start.4) | copy-done | bytes 16777240
  272.4 4.6 %and_convert_fusion.khot_ref = bf16[8192,128]{1,0:T(8,128)(2,1)} fusion(s32[128]{0:T(128)S(1)} %and_select_fusion.1, s32[8192]{0:T(1024)S(1)} %bitcast.9, pred[128]{0:T(512)(128)(4,1)S(1)} %get-tuple-element.14), kind=kLoop, calls=%fused_computation.5 | loop fusion | flops 3145728 | bytes 2130560 | tf_op jit(solution)/shard_map/convert_element_type | solution.py:272
  277.1 0.0 all-gather.4.cloned.1.call-done
  277.1 16.0 %multiply_convert_fusion.q_ref = bf16[512,2048]{1,0:T(8,128)(2,1)S(1)} fusion(bf16[4096,2048]{1,0:T(8,128)(2,1)} %all-gather.4.cloned.1.call-done, bf16[512,4096]{1,0:T(8,128)(2,1)} %copy-done, f32[512]{0:T(512)S(1)} %add_rsqrt_fusion), kind=kOutput, calls=%fused_computation.4 | convolution fusion | flops 8598323200 | bytes 23070720 | tf_op jit(solution)/shard_map/dot_general | solution.py:301
  293.1 91.7 %shard_map.75.part = bf16[512,2048]{1,0:T(8,128)(2,1)S(1)} custom-call(s32[16]{0:T(128)S(1)} %compare_select_fusion.3.kind_ref, bf16[512,2048]{1,0:T(8,128)(2,1)S(1)} %multiply_convert_fusion.q_ref, bf16[8192,1024]{1,0:T(8,128)(2,1)} %bitcast.11, bf16[512,128]{1,0:T(8,128)(2,1)S(1)} %and_convert_fusion.1.qhot_ref, ...), custom_call_target="tpu_custom_call" | custom-call | flops 34359738368 | bytes 16777216 | tf_op jit(solution)/shard_map/pallas_call | solution.py:76
  384.8 44.5 %shard_map.76 = bf16[512,4096]{1,0:T(8,128)(2,1)S(1)} custom-call(bf16[512,2048]{1,0:T(8,128)(2,1)S(1)} %shard_map.75.part), custom_call_target="tpu_custom_call" | custom-call | bytes 67108864 | tf_op jit(solution)/shard_map/pallas_call | solution.py:142
  429.2 0.0 copy-start.1
  429.2 1.9 copy-done.1
  431.2 0.0 all-gather.8.cloned.1.call-done
  431.2 14.5 %convolution_convert_fusion = bf16[512,2048]{1,0:T(8,128)(2,1)} fusion(bf16[512,4096]{1,0:T(8,128)(2,1)} %copy-done.1, bf16[4096,2048]{1,0:T(8,128)(2,1)} %all-gather.8.cloned.1.call-done), kind=kOutput, calls=%fused_computation.6 | convolution fusion | flops 8590983168 | bytes 23068672 | tf_op jit(solution)/shard_map/dot_general | solution.py:335
  (9 shorter events, 0.1 us)
Async XLA Ops:
  6.5 64.7 %all-gather.6.cloned.1.call-start = ((), (), s32[]{:S(2)}) async-start(), calls=%async_computation.1 | async-start | bytes 10485760 | tf_op jit(solution)/shard_map/all_gather | solution.py:288
  12.3 1.5 copy-start.5
  12.3 2.2 copy-start.2
  12.3 264.8 %all-gather.4.cloned.1.call-start = ((), (), s32[]{:S(2)}) async-start(), calls=%async_computation | async-start | bytes 20971520 | tf_op jit(solution)/shard_map/all_gather | solution.py:289
  13.1 418.1 %all-gather.8.cloned.1.call-start = ((), (), s32[]{:S(2)}) async-start(), calls=%async_computation.2 | async-start | bytes 20971520 | tf_op jit(solution)/shard_map/all_gather | solution.py:337
  13.8 49.5 %copy-start.6 = (f32[16]{0:T(128)S(1)}, f32[16]{0:T(128)}, u32[]{:S(2)}) copy-start(f32[16]{0:T(128)} %param.12) | copy-start | bytes 196
  14.5 53.1 %copy-start.3 = (s32[512]{0:T(512)S(1)}, s32[512]{0:T(512)}, u32[]{:S(2)}) copy-start(s32[512]{0:T(512)} %param.8) | copy-start | bytes 6148
  61.2 2.0 copy-start
  266.7 5.7 %copy-start.4 = (bf16[4,4,512,1024]{3,2,1,0:T(8,128)(2,1)}, bf16[4,4,512,1024]{3,2,1,0:T(8,128)(2,1)S(1)}, u32[]{:S(2)}) copy-start(bf16[4,4,512,1024]{3,2,1,0:T(8,128)(2,1)S(1)} %get-tuple-element.7) | copy-start | bytes 50331652
  429.2 1.9 copy-start.1
Sparse Core Ops, SparseCore 0:
  12.4 58.7 all-gather.5
  72.8 171.1 all-gather.3
  245.5 126.6 all-gather.7

commit v4 on v3

--- a/solution.py
+++ b/solution.py
@@ -173,7 +173,7 @@
         for k, (src, dst) in enumerate(((kv, kv_all), (dom, dom_all))):
             pair.append(pltpu.make_async_remote_copy(
                 src_ref=src if first else dst.at[zz, rr], dst_ref=dst.at[zz, rr],
-                send_sem=send.at[zz, rr, k] if send is x_send or send is c_send else send.at[zz, k],
+                send_sem=send.at[zz, rr, k],
                 recv_sem=recv_sem.at[zz, rr, k], device_id=target, device_id_type=MESH))
         return pair
 
@@ -192,59 +192,48 @@
     keep = [pltpu.make_async_copy(kv, kv_all.at[z, r], local_sem.at[0]),
             pltpu.make_async_copy(dom, dom_all.at[z, r], local_sem.at[1])]
 
-    def up(zz, first=False):
-        return copies(zz, r, up_send, {"ctx": z + 1}, first)
-
-    def down(zz, first=False):
-        return copies(zz, r, down_send, {"ctx": z - 1}, first)
-
-    def to_far(zz, first=False):
-        return copies(zz, r, x_send, {"row": far}, first)
+    def up(zz, rr, first=False):
+        return copies(zz, rr, up_send, {"ctx": z + 1}, first)
+
+    def down(zz, rr, first=False):
+        return copies(zz, rr, down_send, {"ctx": z - 1}, first)
 
     def to_near(zz, rr, first=False):
         return copies(zz, rr, c_send, {"row": near}, first)
 
-    pl.when(above)(lambda: start(up(z, True)))
-    pl.when(below)(lambda: start(down(z, True)))
-    start(to_far(z, True))
+    across = copies(z, r, x_send, {"row": far}, True)
+    start(across)
+    pl.when(above)(lambda: start(up(z, r, True)))
+    pl.when(below)(lambda: start(down(z, r, True)))
     start(to_near(z, r, True))
     for copy in keep:
         copy.start()
     landed(z, far)
+    pl.when(above)(lambda: start(up(z, far)))
+    pl.when(below)(lambda: start(down(z, far)))
     start(to_near(z, far))
     for d in range(1, ctx_count):
-        @pl.when(z >= d)
-        def _():
-            landed(z - d, r)
-            pl.when(above)(lambda: start(up(z - d)))
-            start(to_far(z - d))
-            start(to_near(z - d, r))
-
-        @pl.when(z + d < ctx_count)
-        def _():
-            landed(z + d, r)
-            pl.when(below)(lambda: start(down(z + d)))
-            start(to_far(z + d))
-            start(to_near(z + d, r))
-
-        @pl.when(z >= d)
-        def _():
-            landed(z - d, far)
-            start(to_near(z - d, far))
-
-        @pl.when(z + d < ctx_count)
-        def _():
-            landed(z + d, far)
-            start(to_near(z + d, far))
-    mate_far = (near + 2) % 4
+        for rr in (r, far):
+            @pl.when(z >= d)
+            def _():
+                landed(z - d, rr)
+                pl.when(above)(lambda: start(up(z - d, rr)))
+                start(to_near(z - d, rr))
+
+            @pl.when(z + d < ctx_count)
+            def _():
+                landed(z + d, rr)
+                pl.when(below)(lambda: start(down(z + d, rr)))
+                start(to_near(z + d, rr))
+
+    sent(across)
     for zz in range(ctx_count):
         landed(zz, near)
-        landed(zz, mate_far)
-        sent(to_far(zz))
-        sent(to_near(zz, r))
-        sent(to_near(zz, far))
-        pl.when(above & (z >= zz))(lambda zz=zz: sent(up(zz)))
-        pl.when(below & (z <= zz))(lambda zz=zz: sent(down(zz)))
+        landed(zz, (near + 2) % 4)
+        for rr in (r, far):
+            sent(to_near(zz, rr))
+            pl.when(above & (z >= zz))(lambda zz=zz, rr=rr: sent(up(zz, rr)))
+            pl.when(below & (z <= zz))(lambda zz=zz, rr=rr: sent(down(zz, rr)))
     for copy in keep:
         copy.wait()
 
@@ -258,7 +247,7 @@
                    jax.ShapeDtypeStruct((ctx_count, 4) + domains.shape, domains.dtype)],
         in_specs=[pl.BlockSpec(memory_space=pltpu.VMEM)] * 2,
         out_specs=[anywhere] * 2,
-        scratch_shapes=[dma((2,)), dma((ctx_count, 2)), dma((ctx_count, 2)), dma((ctx_count, 4, 2)),
+        scratch_shapes=[dma((2,)), dma((ctx_count, 4, 2)), dma((ctx_count, 4, 2)), dma((ctx_count, 4, 2)),
                         dma((ctx_count, 4, 2)), dma((ctx_count, 4, 2))],
         compiler_params=pltpu.CompilerParams(collective_id=name, has_side_effects=True,
                                              vmem_limit_bytes=16 * 1024 * 1024),

time: 455 us -> 431 us (0.947)
  the two profiles are of different devices: /device:TPU:27 before, /device:TPU:7 now
where the time goes in v4:
time: 431 us; the launch traced here: 430 us
  Pallas kernels  349 us (81%)
  matrix products  37.4 us (9%)
  local copies, waits for them, and re-layouts  16.4 us (4%)
  between operations  13.3 us (3%)
  other arithmetic  8.82 us (2%)
  waiting for transfers between devices  5.05 us (1%)
    pallas_call x1, Pallas kernels, gather_keyvals(): pl.pallas_call(functools.partial(spread_body, ctx_count), out_shape=[jax....  164 us
    pallas_call x2, Pallas kernels, gather_columns(): pl.pallas_call(functools.partial(columns_body, col_count), out_shape=jax....  93.1 us
    pallas_call x1, Pallas kernels, attention(): pl.pallas_call(attention_body, grid_spec=pltpu.PrefetchScalarGridSpec(num...  91.6 us
    dot_general x1, matrix products, shards(): jnp.dot(all_heads, lax.all_gather(out_weight, 'row', axis=0, tiled=True),...  14.5 us
    dot_general x1, matrix products, shards(): query_sums = jnp.dot(normed, query_all, preferred_element_type=jnp.float32)  13.7 us
    unnamed x14, local copies, waits for them, and re-layouts  9.72 us
    dot_general x1, matrix products, shards(): pair_sums = jnp.dot(normed, pair_all, preferred_element_type=jnp.float32)  9.18 us
  transfers between devices with their start and end apart: 3, of which 1 were waited for; matrix products, arithmetic and copies ran while one was open for 8% of the time, Pallas kernels for 81%

profile of v4, /device:TPU:7, one launch (start us, length us, event | category | flops | bytes accessed | tf_op | source)
XLA Modules:
  0.0 429.8 jit_solution(11735104121866754120)
XLA Ops:
  6.5 0.0 all-gather.6.cloned.1.call-start
  6.5 3.0 constant_dynamic-slice_fusion
  9.6 2.7 reshape.165
  12.3 0.0 all-gather.6.cloned.1.call-update
  12.3 0.0 copy-start.5
  12.3 0.0 copy-start.2
  12.3 0.0 all-gather.4.cloned.1.call-start
  12.4 0.7 all-gather.4.cloned.1.call-update
  13.1 0.0 all-gather.8.cloned.1.call-start
  13.1 0.7 all-gather.8.cloned.1.call-update
  13.8 0.0 copy-start.6
  13.8 0.0 copy-done.5
  13.9 0.1 select_reduce_fusion
  14.0 0.6 slice.4
  14.5 0.0 copy-done.2
  14.5 0.0 copy-start.3
  14.5 46.7 %shard_map.73 = bf16[512,4096]{1,0:T(8,128)(2,1)S(1)} custom-call(bf16[512,2048]{1,0:T(8,128)(2,1)S(1)} %copy-done.2), custom_call_target="tpu_custom_call" | custom-call | bytes 67108864 | tf_op jit(solution)/shard_map/pallas_call | solution.py:142
  61.2 0.0 copy-start
  61.2 2.0 copy-done
  63.3 0.0 copy-done.6
  63.3 0.1 broadcast_in_dim.93
  63.4 0.1 broadcast_in_dim.90
  63.5 0.1 copy.11
  63.7 0.1 select_reduce_fusion.1
  63.8 0.6 compare_select_fusion.3.kind_ref
  64.5 3.1 fusion
  67.5 0.1 select_select_fusion.bias_ref
  67.6 0.0 copy-done.3
  67.6 0.1 and_convert_fusion.1.qhot_ref
  67.8 3.7 all-gather.6.cloned.1.call-done
  71.4 9.2 %fusion.5.kv = bf16[512,1024]{1,0:T(8,128)(2,1)S(1)} fusion(bf16[4096,1024]{1,0:T(8,128)(2,1)} %all-gather.6.cloned.1.call-done, bf16[512,4096]{1,0:T(8,128)(2,1)} %copy-done, f32[512]{0:T(512)S(1)} %add_rsqrt_fusion), kind=kOutput, calls=%fused_computation.8 | convolution fusion | flops 4301783040 | bytes 13633536 | tf_op jit(solution)/shard_map/dot_general | solution.py:285
  80.6 164.0 %shard_map.74 = (bf16[4,4,512,1024]{3,2,1,0:T(8,128)(2,1)S(1)}, s32[4,4,4,128]{3,2,1,0:T(4,128)S(1)}) custom-call(bf16[512,1024]{1,0:T(8,128)(2,1)S(1)} %fusion.5.kv, s32[4,128]{1,0:T(4,128)S(1)} %bitcast.10), custom_call_target="tpu_custom_call" | custom-call | bytes 134217728 | tf_op jit(solution)/shard_map/pallas_call | solution.py:244
  244.6 0.0 copy-start.4
  244.6 5.7 %copy-done.4 = bf16[4,4,512,1024]{3,2,1,0:T(8,128)(2,1)} copy-done((bf16[4,4,512,1024]{3,2,1,0:T(8,128)(2,1)}, bf16[4,4,512,1024]{3,2,1,0:T(8,128)(2,1)S(1)}, u32[]{:S(2)}) %copy-start.4) | copy-done | bytes 16777240
  250.3 4.6 %and_convert_fusion.khot_ref = bf16[8192,128]{1,0:T(8,128)(2,1)} fusion(s32[128]{0:T(128)S(1)} %and_select_fusion.1, s32[8192]{0:T(1024)S(1)} %bitcast.9, pred[128]{0:T(512)(128)(4,1)S(1)} %get-tuple-element.14), kind=kLoop, calls=%fused_computation.5 | loop fusion | flops 3145728 | bytes 2130560 | tf_op jit(solution)/shard_map/convert_element_type | solution.py:261
  255.0 0.0 all-gather.4.cloned.1.call-done
  255.0 13.7 %multiply_convert_fusion.q_ref = bf16[512,2048]{1,0:T(8,128)(2,1)S(1)} fusion(bf16[4096,2048]{1,0:T(8,128)(2,1)} %all-gather.4.cloned.1.call-done, bf16[512,4096]{1,0:T(8,128)(2,1)} %copy-done, f32[512]{0:T(512)S(1)} %add_rsqrt_fusion), kind=kOutput, calls=%fused_computation.4 | convolution fusion | flops 8598323200 | bytes 23070720 | tf_op jit(solution)/shard_map/dot_general | solution.py:290
  268.7 91.6 %shard_map.75.part = bf16[512,2048]{1,0:T(8,128)(2,1)S(1)} custom-call(s32[16]{0:T(128)S(1)} %compare_select_fusion.3.kind_ref, bf16[512,2048]{1,0:T(8,128)(2,1)S(1)} %multiply_convert_fusion.q_ref, bf16[8192,1024]{1,0:T(8,128)(2,1)} %bitcast.11, bf16[512,128]{1,0:T(8,128)(2,1)S(1)} %and_convert_fusion.1.qhot_ref, ...), custom_call_target="tpu_custom_call" | custom-call | flops 34359738368 | bytes 16777216 | tf_op jit(solution)/shard_map/pallas_call | solution.py:76
  360.3 46.5 %shard_map.76 = bf16[512,4096]{1,0:T(8,128)(2,1)S(1)} custom-call(bf16[512,2048]{1,0:T(8,128)(2,1)S(1)} %shard_map.75.part), custom_call_target="tpu_custom_call" | custom-call | bytes 67108864 | tf_op jit(solution)/shard_map/pallas_call | solution.py:142
  406.8 0.0 copy-start.1
  406.8 1.9 copy-done.1
  408.7 0.0 all-gather.8.cloned.1.call-done
  408.7 14.5 %convolution_convert_fusion = bf16[512,2048]{1,0:T(8,128)(2,1)} fusion(bf16[512,4096]{1,0:T(8,128)(2,1)} %copy-done.1, bf16[4096,2048]{1,0:T(8,128)(2,1)} %all-gather.8.cloned.1.call-done), kind=kOutput, calls=%fused_computation.6 | convolution fusion | flops 8590983168 | bytes 23068672 | tf_op jit(solution)/shard_map/dot_general | solution.py:324
  (9 shorter events, 0.1 us)
Async XLA Ops:
  6.5 64.9 %all-gather.6.cloned.1.call-start = ((), (), s32[]{:S(2)}) async-start(), calls=%async_computation.1 | async-start | bytes 10485760 | tf_op jit(solution)/shard_map/all_gather | solution.py:277
  12.3 1.5 copy-start.5
  12.3 2.2 copy-start.2
  12.3 242.7 %all-gather.4.cloned.1.call-start = ((), (), s32[]{:S(2)}) async-start(), calls=%async_computation | async-start | bytes 20971520 | tf_op jit(solution)/shard_map/all_gather | solution.py:278
  13.1 395.7 %all-gather.8.cloned.1.call-start = ((), (), s32[]{:S(2)}) async-start(), calls=%async_computation.2 | async-start | bytes 20971520 | tf_op jit(solution)/shard_map/all_gather | solution.py:326
  13.8 49.5 %copy-start.6 = (f32[16]{0:T(128)S(1)}, f32[16]{0:T(128)}, u32[]{:S(2)}) copy-start(f32[16]{0:T(128)} %param.12) | copy-start | bytes 196
  14.5 53.1 %copy-start.3 = (s32[512]{0:T(512)S(1)}, s32[512]{0:T(512)}, u32[]{:S(2)}) copy-start(s32[512]{0:T(512)} %param.8) | copy-start | bytes 6148
  61.2 2.0 copy-start
  244.6 5.7 %copy-start.4 = (bf16[4,4,512,1024]{3,2,1,0:T(8,128)(2,1)}, bf16[4,4,512,1024]{3,2,1,0:T(8,128)(2,1)S(1)}, u32[]{:S(2)}) copy-start(bf16[4,4,512,1024]{3,2,1,0:T(8,128)(2,1)S(1)} %get-tuple-element.7) | copy-start | bytes 50331652
  406.8 1.9 copy-start.1
Sparse Core Ops, SparseCore 0:
  12.4 58.9 all-gather.5
  73.0 125.9 all-gather.3
  200.6 105.6 all-gather.7
